TPU v7x, 32 devices: a whole 2x2x4 slice. The times are simulated.
32 devices in a mesh: rep: 2 (over core), exp: 16 (over z, y, x).
Axes of the slice: x: 2, y: 2, z: 4, core: 2. Of those that a mesh axis runs over, the one named last changes fastest.
Arguments:
- tokens: bfloat16 [25216, 768], P(('rep', 'exp')), may hold values from -6 to 6
- ln1_gain: bfloat16 [768], P('exp'), may hold values from 0.5 to 1.5
- ln1_bias: bfloat16 [768], P('exp'), may hold values from -1.25 to 1.25
- qkv_weight: bfloat16 [768, 2304], P('exp'), may hold values from -0.21875 to 0.21875
- out_weight: bfloat16 [768, 768], P('exp'), may hold values from -0.875 to 0.875
- ln2_gain: bfloat16 [768], P('exp'), may hold values from 0.5 to 1.5
- ln2_bias: bfloat16 [768], P('exp'), may hold values from -1.25 to 1.25
- router_weight: bfloat16 [768, 16], P('exp'), may hold values from -0.21875 to 0.21875
- expert_in: bfloat16 [16, 768, 3072], P('exp'), may hold values from -0.21875 to 0.21875
- expert_out: bfloat16 [16, 3072, 768], P('exp'), may hold values from -2.5 to 2.5
- expert_ids: int32 [25216, 2], P(('rep', 'exp')), may hold values from 0 to 15, as said below
- slot_ids: int32 [25216, 2], P(('rep', 'exp')), may hold values from 0 to 127, as said below
- dropped: int32 [25216, 2], P(('rep', 'exp')), may hold values from 0 to 1, as said below
- cotangent: bfloat16 [25216, 768], P(('rep', 'exp')), may hold values from -6 to 6
Outputs:
- mixed: bfloat16 [25216, 768], P(('rep', 'exp'))
- grad_tokens: float32 [25216, 768], P(('rep', 'exp'))
- grad_ln1_gain: float32 [768], P('exp')
- grad_ln1_bias: float32 [768], P('exp')
- grad_qkv: float32 [768, 2304], P('exp')
- grad_out_weight: float32 [768, 768], P('exp')
- grad_ln2_gain: float32 [768], P('exp')
- grad_ln2_bias: float32 [768], P('exp')
- grad_router: float32 [768, 16], P('exp')
- grad_expert_in: float32 [16, 768, 3072], P('exp')
- grad_expert_out: float32 [16, 3072, 768], P('exp')
Inputs may be any that keep to these rules, and one draw needn't show every extreme that they name: `expert_ids`: each token names 2 different experts. `slot_ids`: slots count a device's earlier routes to the same expert, tokens in order and a token's routes in order; 0 where dropped; in the rows of each device some expert is named by more than 128 routes. `dropped`: 1 exactly where that count reaches 128.
All inputs are finite; a program needn't handle non-finite values.
Results may differ from a plain program's by a relative error of at most 0.018.
Values may be sent and summed in bfloat16 or wider, within the bound.
A program may use at most 256 MiB of HBM per device.

v0:
```python
import jax
import jax.numpy as jnp
from jax import lax
from jax.sharding import PartitionSpec as P

HEADS = 12
HEAD = 64
TOP = 2
SEQ = 197


epsilon = 1e-06


def layer_norm(values, gain, offset):
    centre = jnp.mean(values, axis=-1, keepdims=True)
    centred = values - centre
    spread = jnp.mean(centred * centred, axis=-1, keepdims=True)
    return centred * lax.rsqrt(spread + epsilon) * gain + offset


def gelu_exact(values):
    return jax.nn.gelu(values, approximate=False)


def matmul_tn(left, right):
    return lax.dot_general(
        left, right, (((0,), (0,)), ((), ())), preferred_element_type=jnp.float32
    )


def matmul_nt(left, right):
    return lax.dot_general(
        left, right, (((1,), (1,)), ((), ())), preferred_element_type=jnp.float32
    )


def on_device(
    tokens,
    ln1_gain,
    ln1_bias,
    qkv_weight,
    out_weight,
    ln2_gain,
    ln2_bias,
    router_weight,
    expert_in,
    expert_out,
    expert_ids,
    slot_ids,
    dropped,
    cotangent,
):
    tok_rows, width = tokens.shape
    n_images = tok_rows // SEQ
    scale = HEAD ** (-0.5)
    local_experts = expert_in.shape[0]
    exp_devices = lax.axis_size("exp")
    num_experts = exp_devices * local_experts
    capacity = (5 * TOP * tok_rows // (4 * num_experts) + 7) // 8 * 8
    slot_total = num_experts * capacity
    fetched = (
        lax.all_gather(qkv_weight, "exp", axis=0, tiled=True),
        lax.all_gather(out_weight, "exp", axis=0, tiled=True),
        lax.all_gather(router_weight, "exp", axis=0, tiled=True),
        lax.all_gather(ln1_gain, "exp", axis=0, tiled=True),
        lax.all_gather(ln1_bias, "exp", axis=0, tiled=True),
        lax.all_gather(ln2_gain, "exp", axis=0, tiled=True),
        lax.all_gather(ln2_bias, "exp", axis=0, tiled=True),
    )
    w_qkv, w_attn, w_router = (fetched[0], fetched[1], fetched[2])
    gain_one = fetched[3].astype(jnp.float32)
    bias_one = fetched[4].astype(jnp.float32)
    gain_two = fetched[5].astype(jnp.float32)
    bias_two = fetched[6].astype(jnp.float32)
    inputs = tokens.astype(jnp.float32)
    normed1 = layer_norm(inputs, gain_one, bias_one).astype(jnp.bfloat16)
    qkv_low = jnp.dot(normed1, w_qkv, preferred_element_type=jnp.float32).astype(jnp.bfloat16)
    queries = qkv_low[:, :width].reshape(n_images, SEQ, HEADS, HEAD)
    keys_all = qkv_low[:, width : 2 * width].reshape(n_images, SEQ, HEADS, HEAD)
    values_all = qkv_low[:, 2 * width :].reshape(n_images, SEQ, HEADS, HEAD)
    scores = (
        jnp.einsum("bqhd,bkhd->bhqk", queries, keys_all, preferred_element_type=jnp.float32) * scale
    )
    log_total = jax.nn.logsumexp(scores, axis=-1, keepdims=True)
    attn_low = jnp.exp(scores - log_total).astype(jnp.bfloat16)
    attended = jnp.einsum(
        "bhqk,bkhd->bqhd", attn_low, values_all, preferred_element_type=jnp.float32
    )
    attended = attended.reshape(tok_rows, width).astype(jnp.bfloat16)
    mid = inputs + jnp.dot(attended, w_attn, preferred_element_type=jnp.float32)
    normed2 = layer_norm(mid, gain_two, bias_two).astype(jnp.bfloat16)
    logits = jnp.dot(normed2, w_router, preferred_element_type=jnp.float32)
    router_probs = jax.nn.softmax(logits, axis=-1)
    onehot = (
        expert_ids[:, :, None] == jnp.arange(num_experts, dtype=jnp.int32)[None, None, :]
    ).astype(jnp.float32)
    keep_mask = (1 - dropped).astype(jnp.float32)
    gates = jnp.sum(onehot * router_probs[:, None, :], axis=-1) * keep_mask
    targets = jnp.where(dropped == 1, slot_total, expert_ids * capacity + slot_ids).reshape(-1)
    safe_slots = jnp.minimum(targets, slot_total - 1)
    spread_rows = jnp.broadcast_to(normed2[:, None, :], (tok_rows, TOP, width)).reshape(-1, width)
    send_buffer = (
        jnp.zeros((slot_total, width), jnp.bfloat16).at[targets].set(spread_rows, mode="drop")
    )
    arrived = lax.all_to_all(
        send_buffer.reshape(num_experts, capacity, width),
        "exp",
        split_axis=0,
        concat_axis=0,
        tiled=True,
    )
    expert_rows = arrived.reshape(exp_devices, local_experts, capacity, width).transpose(1, 0, 2, 3)
    expert_rows = expert_rows.reshape(local_experts, exp_devices * capacity, width)
    pre_act = jnp.einsum("erd,edf->erf", expert_rows, expert_in, preferred_element_type=jnp.float32)
    hidden_low = gelu_exact(pre_act).astype(jnp.bfloat16)
    result_low = jnp.einsum(
        "erf,efd->erd", hidden_low, expert_out, preferred_element_type=jnp.float32
    ).astype(jnp.bfloat16)
    outgoing = result_low.reshape(local_experts, exp_devices, capacity, width).transpose(1, 0, 2, 3)
    returned = lax.all_to_all(
        outgoing.reshape(num_experts, capacity, width),
        "exp",
        split_axis=0,
        concat_axis=0,
        tiled=True,
    )
    back_rows = (
        returned.reshape(slot_total, width)[safe_slots]
        .reshape(tok_rows, TOP, width)
        .astype(jnp.float32)
    )
    moe = jnp.sum(gates[:, :, None] * back_rows, axis=1)
    mixed = (mid + moe).astype(jnp.bfloat16)
    grad_output = cotangent.astype(jnp.float32)
    grad_gates = jnp.sum(grad_output[:, None, :] * back_rows, axis=-1)
    grad_rows = (
        (gates[:, :, None] * grad_output[:, None, :]).astype(jnp.bfloat16).reshape(-1, width)
    )
    grad_buffer = (
        jnp.zeros((slot_total, width), jnp.bfloat16).at[targets].set(grad_rows, mode="drop")
    )
    grad_arrived = lax.all_to_all(
        grad_buffer.reshape(num_experts, capacity, width),
        "exp",
        split_axis=0,
        concat_axis=0,
        tiled=True,
    )
    grad_result = grad_arrived.reshape(exp_devices, local_experts, capacity, width).transpose(
        1, 0, 2, 3
    )
    grad_result = grad_result.reshape(local_experts, exp_devices * capacity, width)
    grad_hidden = jnp.einsum(
        "erd,efd->erf", grad_result, expert_out, preferred_element_type=jnp.float32
    )
    grad_second = jnp.einsum(
        "erf,erd->efd", hidden_low, grad_result, preferred_element_type=jnp.float32
    )
    _, gelu_pull = jax.vjp(gelu_exact, pre_act)
    grad_pre = gelu_pull(grad_hidden)[0].astype(jnp.bfloat16)
    grad_first = jnp.einsum(
        "erd,erf->edf", expert_rows, grad_pre, preferred_element_type=jnp.float32
    )
    grad_sent = jnp.einsum(
        "erf,edf->erd", grad_pre, expert_in, preferred_element_type=jnp.float32
    ).astype(jnp.bfloat16)
    grad_sent = grad_sent.reshape(local_experts, exp_devices, capacity, width).transpose(1, 0, 2, 3)
    grad_home = lax.all_to_all(
        grad_sent.reshape(num_experts, capacity, width),
        "exp",
        split_axis=0,
        concat_axis=0,
        tiled=True,
    )
    grad_picked = (
        grad_home.reshape(slot_total, width)[safe_slots]
        .reshape(tok_rows, TOP, width)
        .astype(jnp.float32)
    )
    grad_normed2 = jnp.sum(keep_mask[:, :, None] * grad_picked, axis=1)
    back_qkv, back_attn, back_router = (w_qkv, w_attn, w_router)
    grad_chosen = grad_gates * keep_mask
    grad_probs = jnp.sum(onehot * grad_chosen[:, :, None], axis=1)
    inner_probs = jnp.sum(grad_probs * router_probs, axis=-1, keepdims=True)
    grad_logits = (router_probs * (grad_probs - inner_probs)).astype(jnp.bfloat16)
    grad_router = matmul_tn(normed2, grad_logits)
    grad_normed2 = grad_normed2 + matmul_nt(grad_logits, back_router)
    _, norm_two_pull = jax.vjp(layer_norm, mid, gain_two, bias_two)
    grad_mid_part, grad_gain_two, grad_bias_two = norm_two_pull(grad_normed2)
    grad_mid = grad_output + grad_mid_part
    grad_mid_low = grad_mid.astype(jnp.bfloat16)
    grad_attn_w = matmul_tn(attended, grad_mid_low)
    grad_attended = (
        matmul_nt(grad_mid_low, back_attn).astype(jnp.bfloat16).reshape(n_images, SEQ, HEADS, HEAD)
    )
    again_scores = (
        jnp.einsum("bqhd,bkhd->bhqk", queries, keys_all, preferred_element_type=jnp.float32) * scale
    )
    soft_again = jnp.exp(again_scores - log_total)
    grad_values = jnp.einsum(
        "bhqk,bqhd->bkhd",
        soft_again.astype(jnp.bfloat16),
        grad_attended,
        preferred_element_type=jnp.float32,
    )
    grad_soft = jnp.einsum(
        "bqhd,bkhd->bhqk", grad_attended, values_all, preferred_element_type=jnp.float32
    )
    row_inner = jnp.sum(grad_soft * soft_again, axis=-1, keepdims=True)
    grad_scores = (soft_again * (grad_soft - row_inner)).astype(jnp.bfloat16)
    grad_queries = (
        jnp.einsum("bhqk,bkhd->bqhd", grad_scores, keys_all, preferred_element_type=jnp.float32)
        * scale
    )
    grad_keys = (
        jnp.einsum("bhqk,bqhd->bkhd", grad_scores, queries, preferred_element_type=jnp.float32)
        * scale
    )
    grad_qkv_rows = jnp.concatenate(
        [
            grad_queries.reshape(tok_rows, width),
            grad_keys.reshape(tok_rows, width),
            grad_values.reshape(tok_rows, width),
        ],
        axis=1,
    ).astype(jnp.bfloat16)
    grad_qkv_w = matmul_tn(normed1, grad_qkv_rows)
    grad_normed1 = matmul_nt(grad_qkv_rows, back_qkv)
    _, norm_one_pull = jax.vjp(layer_norm, inputs, gain_one, bias_one)
    grad_in_part, grad_gain_one, grad_bias_one = norm_one_pull(grad_normed1)
    grad_tokens = grad_mid + grad_in_part
    shares = (
        lax.psum_scatter(grad_qkv_w, "exp", scatter_dimension=0, tiled=True),
        lax.psum_scatter(grad_attn_w, "exp", scatter_dimension=0, tiled=True),
        lax.psum_scatter(grad_router, "exp", scatter_dimension=0, tiled=True),
        lax.psum_scatter(grad_gain_one, "exp", scatter_dimension=0, tiled=True),
        lax.psum_scatter(grad_bias_one, "exp", scatter_dimension=0, tiled=True),
        lax.psum_scatter(grad_gain_two, "exp", scatter_dimension=0, tiled=True),
        lax.psum_scatter(grad_bias_two, "exp", scatter_dimension=0, tiled=True),
    )
    totals = (
        lax.psum(shares[0].astype(jnp.bfloat16), "rep").astype(jnp.float32),
        lax.psum(shares[1].astype(jnp.bfloat16), "rep").astype(jnp.float32),
        lax.psum(shares[2].astype(jnp.bfloat16), "rep").astype(jnp.float32),
        lax.psum(shares[3].astype(jnp.bfloat16), "rep").astype(jnp.float32),
        lax.psum(shares[4].astype(jnp.bfloat16), "rep").astype(jnp.float32),
        lax.psum(shares[5].astype(jnp.bfloat16), "rep").astype(jnp.float32),
        lax.psum(shares[6].astype(jnp.bfloat16), "rep").astype(jnp.float32),
        lax.psum(grad_first.astype(jnp.bfloat16), "rep").astype(jnp.float32),
        lax.psum(grad_second.astype(jnp.bfloat16), "rep").astype(jnp.float32),
    )
    return (
        mixed,
        grad_tokens,
        totals[3],
        totals[4],
        totals[0],
        totals[1],
        totals[5],
        totals[6],
        totals[2],
        totals[7],
        totals[8],
    )


def solution(mesh):
    placed = (
        P(("rep", "exp"), None),
        P("exp"),
        P("exp"),
        P("exp", None),
        P("exp", None),
        P("exp"),
        P("exp"),
        P("exp", None),
        P("exp", None, None),
        P("exp", None, None),
        P(("rep", "exp"), None),
        P(("rep", "exp"), None),
        P(("rep", "exp"), None),
        P(("rep", "exp"), None),
    )
    return jax.shard_map(
        on_device,
        mesh=mesh,
        in_specs=placed,
        out_specs=(
            P(("rep", "exp"), None),
            P(("rep", "exp"), None),
            P("exp"),
            P("exp"),
            P("exp", None),
            P("exp", None),
            P("exp"),
            P("exp"),
            P("exp", None),
            P("exp", None, None),
            P("exp", None, None),
        ),
        check_vma=False,
    )
```

profile of v0, /device:TPU:13, one launch (start us, length us, event | category | flops | bytes accessed | tf_op | source)
XLA Modules:
  0.0 1037.5 jit_solution(10839872498032361687)
XLA Ops:
  14.0 26.1 %all-reduce.9 = (bf16[768]{0:T(1024)(128)(2,1)S(1)}, bf16[768]{0:T(1024)(128)(2,1)S(1)}, bf16[768]{0:T(1024)(128)(2,1)S(1)}, bf16[768]{0:T(1024)(128)(2,1)S(1)}) all-reduce(bf16[768]{0:T(1024)(128)(2,1)S(1)} %dynamic-update-slice.1, bf16[768]{0:T(1024)(128)(2,1)S(1)} %dynamic-update-slice, ...), channel_id=1, replica_groups=mesh['rep'=2,'exp'=16] {'exp'}, use_global_device_ids=true, to_apply=%add.1 | all-reduce | flops 3072 | bytes 12288
  46.1 36.4 %all-gather.4.cloned.1.call-done = bf16[768,2304]{1,0:T(8,128)(2,1)} async-done(((bf16[48,2304]{1,0:T(8,128)(2,1)}), bf16[768,2304]{1,0:T(8,128)(2,1)}) %all-gather.4.cloned.1.call-update) | async-done | bytes 3538960 | tf_op jit(solution)/shard_map/all_gather | solution.py:63
  129.8 9.0 all-gather.6.cloned.1.call-done
  153.0 13.2 %scatter_custom_fusion = bf16[2048,768]{1,0:T(8,128)(2,1)} fusion(s32[1576]{0:T(1024)S(1)} %get-tuple-element.21, bf16[1576,768]{1,0:T(8,128)(2,1)} %reshape.377, bf16[]{:T(256)} %constant.10.clone.1), kind=kCustom, calls=%fused_computation.76 | custom fusion | bytes 3146240 | tf_op jit(solution)/shard_map/scatter | solution.py:104
  171.6 86.7 %all-gather = bf16[16,48,16]{1,2,0:T(8,128)(2,1)S(1)} all-gather(bf16[1,48,16]{1,2,0:T(8,128)(2,1)S(1)} %bitcast.87), channel_id=1, replica_groups=mesh['rep'=2,'exp'=16] {'exp'}, dimensions={0}, use_global_device_ids=true | all-gather | bytes 26112 | tf_op jit(solution)/shard_map/all_gather | solution.py:65
  270.6 19.5 %scatter_custom_fusion.1 = bf16[2048,768]{1,0:T(8,128)(2,1)} fusion(s32[1576]{0:T(1024)S(1)} %get-tuple-element.21, f32[1576,768]{1,0:T(8,128)} %mul.282, f32[1576]{0:T(1024)S(1)} %mul.279, bf16[]{:T(256)} %constant.10.clone.1), kind=kCustom, calls=%fused_computation.70 | custom fusion | flops 2420736 | bytes 7995394 | tf_op jit(solution)/shard_map/scatter | solution.py:141
  295.9 64.0 %multiply_convert_fusion = (bf16[2048,3072]{1,0:T(8,128)(2,1)S(1)}, f32[2048,3072]{1,0:T(8,128)}, f32[2048,3072]{1,0:T(8,128)}) fusion(bf16[2048,768]{1,0:T(8,128)(2,1)} %bitcast.4, bf16[1,768,3072]{2,1,0:T(8,128)(2,1)} %param.22), kind=kOutput, calls=%fused_computation.7 | convolution fusion | flops 10072621056 | bytes 70778880 | tf_op jit(solution)/shard_map/erd,edf->erf/dot_general | solution.py:115
  364.3 11.3 %fusion.23 = bf16[2048,768]{1,0:T(8,128)(2,1)} fusion(bf16[2048,3072]{1,0:T(8,128)(2,1)S(1)} %get-tuple-element.41, bf16[1,3072,768]{2,1,0:T(8,128)(2,1)S(1)} %copy-done.61), kind=kOutput, calls=%fused_computation.53 | convolution fusion | flops 9665249280 | bytes 20447232 | tf_op jit(solution)/shard_map/erf,efd->erd/dot_general | solution.py:117
  382.2 33.0 %add_convert_fusion = bf16[2048,3072]{1,0:T(8,128)(2,1)} fusion(f32[2048,3072]{1,0:T(8,128)} %get-tuple-element.42, f32[2048,3072]{1,0:T(8,128)} %get-tuple-element.55, bf16[2048,768]{1,0:T(8,128)(2,1)} %bitcast.10, bf16[1,3072,768]{2,1,0:T(8,128)(2,1)} %param.23), kind=kOutput, calls=%fused_computation.6 | convolution fusion | flops 9751756800 | bytes 70778880 | tf_op jit(solution)/shard_map/erd,efd->erf/dot_general | solution.py:154
  415.3 15.4 %fusion.20 = bf16[2048,768]{1,0:T(8,128)(2,1)} fusion(bf16[2048,3072]{1,0:T(8,128)(2,1)} %add_convert_fusion, bf16[1,768,3072]{2,1,0:T(8,128)(2,1)} %param.22), kind=kOutput, calls=%fused_computation.52 | convolution fusion | flops 9665249280 | bytes 20447232 | tf_op jit(solution)/shard_map/erf,edf->erd/dot_general | solution.py:165
  430.7 21.4 %all-to-all-done.1 = bf16[16,128,768]{2,1,0:T(8,128)(2,1)S(1)} async-done(((bf16[16,128,768]{2,1,0:T(8,128)(2,1)}), bf16[16,128,768]{2,1,0:T(8,128)(2,1)S(1)}, u32[]{:S(2)}, u32[]{:S(2)}) %all-to-all-start.1) | async-done | bytes 3145760 | tf_op jit(solution)/shard_map/all_to_all | solution.py:121
  462.8 10.2 gather_fusion
  479.4 14.0 %multiply_reduce_fusion.2 = (f32[788,2]{1,0:T(8,128)}, f32[788,768]{1,0:T(8,128)}) fusion(f32[788,2,768]{2,1,0:T(2,128)} %reshape.355, f32[788,768]{1,0:T(8,128)} %convert_element_type.174, f32[788,2]{1,0:T(8,128)S(1)} %copy-done.23), kind=kLoop, calls=%fused_computation.30 | loop fusion | flops 4234712 | bytes 9695552 | tf_op jit(solution)/shard_map/reduce_sum | solution.py:136
  497.7 31.0 %all-to-all-done.3 = bf16[16,128,768]{2,1,0:T(8,128)(2,1)S(1)} async-done(((bf16[16,128,768]{2,1,0:T(8,128)(2,1)}), bf16[16,128,768]{2,1,0:T(8,128)(2,1)S(1)}, u32[]{:S(2)}, u32[]{:S(2)}) %all-to-all-start.3) | async-done | bytes 3145760 | tf_op jit(solution)/shard_map/all_to_all | solution.py:169
  541.7 9.8 multiply_reduce_fusion.3
  584.6 7.6 multiply_reduce_fusion
  592.2 11.8 %multiply_convert_fusion.1 = bf16[4,12,197,197]{2,3,1,0:T(8,128)(2,1)} fusion(f32[4,12,197,197]{2,3,1,0:T(8,128)} %get-tuple-element.60, f32[4,12,197,197]{2,3,1,0:T(8,128)} %copy-done, f32[4,12,197]{2,1,0:T(8,128)S(1)} %get-tuple-element.59, f32[4,12,197]{2,1,0:T(8,128)S(1)} %copy-done.25), kind=kLoop, calls=%fused_computation.21 | loop fusion | flops 9314160 | bytes 18703968 | tf_op jit(solution)/shard_map/convert_element_type | solution.py:211
  628.4 15.4 %fusion.14 = bf16[1,768,3072]{2,1,0:T(8,128)(2,1)} fusion(bf16[2048,768]{1,0:T(8,128)(2,1)} %bitcast.4, bf16[2048,3072]{1,0:T(8,128)(2,1)} %add_convert_fusion), kind=kOutput, calls=%fused_computation.41 | convolution fusion | flops 9666035712 | bytes 20447232 | tf_op jit(solution)/shard_map/erd,erf->edf/dot_general | solution.py:162
  645.2 15.6 %fusion.15 = bf16[1,3072,768]{2,1,0:T(8,128)(2,1)} fusion(bf16[2048,3072]{1,0:T(8,128)(2,1)} %copy-done.62, bf16[2048,768]{1,0:T(8,128)(2,1)} %bitcast.10), kind=kOutput, calls=%fused_computation.42 | convolution fusion | flops 9666035712 | bytes 20447232 | tf_op jit(solution)/shard_map/erf,erd->efd/dot_general | solution.py:157
  660.8 26.9 %reduce-scatter.8.cloned.1.call-done = f32[48,768]{1,0:T(8,128)} async-done(((f32[768,768]{1,0:T(8,128)}), f32[48,768]{1,0:T(8,128)}) %reduce-scatter.8.cloned.1.call-update) | async-done | bytes 147472 | tf_op jit(solution)/shard_map/reduce_scatter | solution.py:235
  689.3 154.2 %reduce-scatter.6.cloned.1.call-done = f32[48,2304]{1,0:T(8,128)} async-done(((f32[768,2304]{1,0:T(8,128)}), f32[48,2304]{1,0:T(8,128)}) %reduce-scatter.6.cloned.1.call-update) | async-done | bytes 442384 | tf_op jit(solution)/shard_map/reduce_scatter | solution.py:234
  855.6 52.2 %all-reduce.8 = (bf16[768]{0:T(1024)(128)(2,1)S(1)}, bf16[768]{0:T(1024)(128)(2,1)S(1)}, bf16[768]{0:T(1024)(128)(2,1)S(1)}, bf16[768]{0:T(1024)(128)(2,1)S(1)}) all-reduce(f32[768]{0:T(1024)S(1)} %get-tuple-element.15, f32[768]{0:T(1024)S(1)} %get-tuple-element.18, ...), channel_id=2, replica_groups=mesh['rep'=2,'exp'=16] {'exp'}, use_global_device_ids=true, to_apply=%region_22.23.clone | all-reduce | flops 3072 | bytes 18432
  912.1 57.7 %reduce-scatter.10.cloned.1.call-done = f32[48,16]{1,0:T(8,128)} async-done(((f32[768,16]{1,0:T(8,128)}), f32[48,16]{1,0:T(8,128)}) %reduce-scatter.10.cloned.1.call-update) | async-done | bytes 3088
  977.8 39.2 %all-reduce.14.cloned.1.call-done = (bf16[48,2304]{1,0:T(8,128)(2,1)}, bf16[48,768]{1,0:T(8,128)(2,1)}, bf16[1,768,3072]{2,1,0:T(8,128)(2,1)}, bf16[1,3072,768]{2,1,0:T(8,128)(2,1)}) async-done(((bf16[48,2304]{1,0:T(8,128)(2,1)}, bf16[48,768]{1,0:T(8,128)(2,1)}, bf16[1,768,3072]{2,1,0:T(8,128)(2,1)}, bf16[1,3072,768]{2,1,0:T(8,128)(2,1)}), (bf16[48,2304]{1,0:T(8,128)(2,1)}, bf16[48,768]{1,0:T(8,128)(2,1)}, ...) | async-done | bytes 9732112 | tf_op jit(solution)/shard_map/psum | solution.py:243
  (253 shorter events, 239.3 us)
Async XLA Ops:
  7.2 75.3 %copy-start.6 = (bf16[788,768]{1,0:T(8,128)(2,1)S(1)}, bf16[788,768]{1,0:T(8,128)(2,1)}, u32[]{:S(2)}) copy-start(bf16[788,768]{1,0:T(8,128)(2,1)} %param.14) | copy-start | bytes 3631108
  7.2 75.2 %all-gather.4.cloned.1.call-start = ((), (), s32[]{:S(2)}) async-start(), calls=%async_computation.7 | async-start | bytes 3760128 | tf_op jit(solution)/shard_map/all_gather | solution.py:63
  7.9 130.8 %all-gather.6.cloned.1.call-start = ((), (), s32[]{:S(2)}) async-start(), calls=%async_computation.8 | async-start | bytes 1253376 | tf_op jit(solution)/shard_map/all_gather | solution.py:64
  40.2 42.2 %copy-start.52 = (f32[768]{0:T(1024)}, f32[768]{0:T(1024)S(1)}, u32[]{:S(2)}) copy-start(f32[768]{0:T(1024)S(1)} %convert_element_type.157) | copy-start | bytes 9220
  40.2 42.2 %copy-start.59 = (f32[768]{0:T(1024)}, f32[768]{0:T(1024)S(1)}, u32[]{:S(2)}) copy-start(f32[768]{0:T(1024)S(1)} %convert_element_type.158) | copy-start | bytes 9220
  41.8 40.7 %copy-start.40 = (f32[788]{0:T(1024)}, f32[788]{0:T(1024)S(1)}, u32[]{:S(2)}) copy-start(f32[788]{0:T(1024)S(1)} %broadcast_multiply_fusion.1) | copy-start | bytes 9460
  43.6 38.8 %copy-start.54 = (f32[788]{0:T(1024)}, f32[788]{0:T(1024)S(1)}, u32[]{:S(2)}) copy-start(f32[788]{0:T(1024)S(1)} %fusion.51) | copy-start | bytes 9460
  43.6 98.7 %copy-start.42 = (f32[768]{0:T(1024)}, f32[768]{0:T(1024)S(1)}, u32[]{:S(2)}) copy-start(f32[768]{0:T(1024)S(1)} %convert_element_type.165) | copy-start | bytes 9220
  143.7 125.4 %copy-start.4 = (bf16[788,768]{1,0:T(8,128)(2,1)}, bf16[788,768]{1,0:T(8,128)(2,1)S(1)}, u32[]{:S(2)}) copy-start(bf16[788,768]{1,0:T(8,128)(2,1)S(1)} %add_convert_fusion.2) | copy-start | bytes 3631108
  166.2 92.3 %copy-start.12 = (bf16[788,768]{1,0:T(8,128)(2,1)S(1)}, bf16[788,768]{1,0:T(8,128)(2,1)}, u32[]{:S(2)}) copy-start(bf16[788,768]{1,0:T(8,128)(2,1)} %param.27) | copy-start | bytes 3631108
  166.2 123.9 %all-to-all-start = ((bf16[16,128,768]{2,1,0:T(8,128)(2,1)}), bf16[16,128,768]{2,1,0:T(8,128)(2,1)}, u32[]{:S(2)}, u32[]{:S(2)}) async-start(bf16[16,128,768]{2,1,0:T(8,128)(2,1)} %bitcast.84), calls=%async_computation | async-start | bytes 6291456 | tf_op jit(solution)/shard_map/all_to_all | solution.py:106
  269.5 20.6 %copy-start.33 = (f32[788]{0:T(1024)}, f32[788]{0:T(1024)S(1)}, u32[]{:S(2)}) copy-start(f32[788]{0:T(1024)S(1)} %get-tuple-element.56) | copy-start | bytes 9460
  270.3 19.8 %copy-start.22 = (f32[788,2]{1,0:T(8,128)}, f32[788,2]{1,0:T(8,128)S(1)}, u32[]{:S(2)}) copy-start(f32[788,2]{1,0:T(8,128)S(1)} %copy.111) | copy-start | bytes 18916
  290.1 85.5 %all-to-all-start.2 = ((bf16[16,128,768]{2,1,0:T(8,128)(2,1)}), bf16[16,128,768]{2,1,0:T(8,128)(2,1)}, u32[]{:S(2)}, u32[]{:S(2)}) async-start(bf16[16,128,768]{2,1,0:T(8,128)(2,1)} %bitcast.9), calls=%async_computation.2 | async-start | bytes 6291456 | tf_op jit(solution)/shard_map/all_to_all | solution.py:143
  295.9 68.4 %copy-start.61 = (bf16[1,3072,768]{2,1,0:T(8,128)(2,1)S(1)}, bf16[1,3072,768]{2,1,0:T(8,128)(2,1)}, u32[]{:S(2)}) copy-start(bf16[1,3072,768]{2,1,0:T(8,128)(2,1)} %param.23) | copy-start | bytes 14155780
  375.6 76.5 %all-to-all-start.1 = ((bf16[16,128,768]{2,1,0:T(8,128)(2,1)}), bf16[16,128,768]{2,1,0:T(8,128)(2,1)S(1)}, u32[]{:S(2)}, u32[]{:S(2)}) async-start(bf16[16,128,768]{2,1,0:T(8,128)(2,1)} %bitcast.86), calls=%async_computation.1 | async-start | bytes 6291456 | tf_op jit(solution)/shard_map/all_to_all | solution.py:121
  453.8 74.9 %all-to-all-start.3 = ((bf16[16,128,768]{2,1,0:T(8,128)(2,1)}), bf16[16,128,768]{2,1,0:T(8,128)(2,1)S(1)}, u32[]{:S(2)}, u32[]{:S(2)}) async-start(bf16[16,128,768]{2,1,0:T(8,128)(2,1)} %bitcast.85), calls=%async_computation.3 | async-start | bytes 6291456 | tf_op jit(solution)/shard_map/all_to_all | solution.py:169
  458.3 229.5 %reduce-scatter.8.cloned.1.call-start = ((), (), s32[]{:S(2)}) async-start(), calls=%async_computation.10 | async-start | bytes 2506752 | tf_op jit(solution)/shard_map/reduce_scatter | solution.py:235
  479.4 16.6 %copy-start.34 = (f32[788]{0:T(1024)S(1)}, f32[788]{0:T(1024)}, u32[]{:S(2)}) copy-start(f32[788]{0:T(1024)} %copy-done.33) | copy-start | bytes 9460
  561.3 282.2 %reduce-scatter.6.cloned.1.call-start = ((), (), s32[]{:S(2)}) async-start(), calls=%async_computation.9 | async-start | bytes 7520256 | tf_op jit(solution)/shard_map/reduce_scatter | solution.py:234
  628.3 15.5 %copy-start.5 = (bf16[788,768]{1,0:T(8,128)(2,1)S(1)}, bf16[788,768]{1,0:T(8,128)(2,1)}, u32[]{:S(2)}) copy-start(bf16[788,768]{1,0:T(8,128)(2,1)} %copy-done.4) | copy-start | bytes 3631108
  628.3 341.6 %reduce-scatter.10.cloned.1.call-start = ((), (), s32[]{:S(2)}) async-start(), calls=%async_computation.11 | async-start | bytes 417792
  645.1 371.9 %all-reduce.14.cloned.1.call-start = ((), (), s32[]{:S(2)}) async-start(), calls=%async_computation.12 | async-start | bytes 19464192 | tf_op jit(solution)/shard_map/psum | solution.py:243
  853.0 55.1 %copy-start.15 = (bf16[788,768]{1,0:T(8,128)(2,1)S(1)}, bf16[788,768]{1,0:T(8,128)(2,1)}, u32[]{:S(2)}) copy-start(bf16[788,768]{1,0:T(8,128)(2,1)} %param.27) | copy-start | bytes 3631108
  (49 other events, 220.2 us)
Sparse Core Ops, SparseCore 0:
  10.8 71.5 all-gather.3
  85.2 53.5 all-gather.5
  561.4 126.3 reduce-scatter.7
  694.4 149.0 reduce-scatter.5
  849.3 120.5 reduce-scatter.9
  973.7 43.2 all-reduce.13
where the time goes:
time: 1050 us; the launch traced here: 1040 us
  waiting for transfers between devices  377 us (36%)
  matrix products  215 us (20%)
  blocking collectives  169 us (16%)
  local copies, waits for them, and re-layouts  140 us (13%)
  other arithmetic  96.5 us (9%)
  starting transfers between devices  22.5 us (2%)
  between operations  16.4 us (2%)
    reduce_scatter x1, waiting for transfers between devices, on_device(): lax.psum_scatter(grad_qkv_w, 'exp', scatter_dimension=0, tiled=True)  154 us
    all_gather x1, blocking collectives, on_device(): lax.all_gather(router_weight, 'exp', axis=0, tiled=True)  86.7 us
    unnamed x2, blocking collectives  78.3 us
    dot_general x1, matrix products, on_device(): jnp.einsum('erd,edf->erf', expert_rows, expert_in, preferred_element_type...  64 us
    unnamed x7, waiting for transfers between devices  59.2 us
    psum x1, waiting for transfers between devices, on_device(): lax.psum(shares[0].astype(jnp.bfloat16), 'rep').astype(jnp.float32)  39.2 us
    all_gather x1, waiting for transfers between devices, on_device(): lax.all_gather(qkv_weight, 'exp', axis=0, tiled=True)  36.4 us
    dot_general x1, matrix products, on_device(): jnp.einsum('erd,efd->erf', grad_result, expert_out, preferred_element_typ...  33 us
  transfers between devices with their start and end apart: 10, of which 8 were waited for; matrix products, arithmetic and copies ran while one was open for 35% of the time, Pallas kernels for 0%

commit v1 on v0

v1 whole, which is shorter than its diff:
```python
import functools

import jax
import jax.numpy as jnp
from jax import lax
from jax.experimental import pallas as pl
from jax.experimental.pallas import tpu as pltpu
from jax.sharding import PartitionSpec as P

HEADS = 12
HEAD = 64
TOP = 2
SEQ = 197
SEQ_PAD = 208
PAIR = 2 * HEAD


epsilon = 1e-06


def layer_norm(values, gain, offset):
    centre = jnp.mean(values, axis=-1, keepdims=True)
    centred = values - centre
    spread = jnp.mean(centred * centred, axis=-1, keepdims=True)
    return centred * lax.rsqrt(spread + epsilon) * gain + offset


def gelu_and_slope(values):
    size = jnp.abs(values) * 0.7071067811865476
    step = 1.0 / (1.0 + 0.3275911 * size)
    decay = jnp.exp(-(size * size))
    poly = step * (
        0.254829592
        + step * (-0.284496736 + step * (1.421413741 + step * (-1.453152027 + step * 1.061405429)))
    )
    tail = 0.5 * poly * decay
    cdf = jnp.where(values < 0, tail, 1.0 - tail)
    return values * cdf, cdf + values * decay * 0.3989422804014327


def matmul_tn(left, right):
    return lax.dot_general(
        left, right, (((0,), (0,)), ((), ())), preferred_element_type=jnp.float32
    )


def matmul_nt(left, right):
    return lax.dot_general(
        left, right, (((1,), (1,)), ((), ())), preferred_element_type=jnp.float32
    )


def head_lanes(first):
    lanes = lax.broadcasted_iota(jnp.int32, (SEQ_PAD, PAIR), 1)
    return (lanes < HEAD) if first else (lanes >= HEAD)


def head_probs(queries, keys):
    scores = matmul_nt(queries, keys) * HEAD ** (-0.5)
    columns = lax.broadcasted_iota(jnp.int32, (SEQ_PAD, SEQ_PAD), 1)
    scores = jnp.where(columns < SEQ, scores, -1e30)
    powers = jnp.exp(scores - jnp.max(scores, axis=-1, keepdims=True))
    return powers * (1.0 / jnp.sum(powers, axis=-1, keepdims=True))


def attend_kernel(width, qkv_ref, out_ref):
    for pair in range(width // PAIR):
        at = pair * PAIR
        queries = qkv_ref[0, :, at : at + PAIR]
        keys = qkv_ref[0, :, width + at : width + at + PAIR]
        values = qkv_ref[0, :, 2 * width + at : 2 * width + at + PAIR]
        result = None
        for first in (True, False):
            lanes = head_lanes(first)
            mine = jnp.where(lanes, queries, jnp.zeros_like(queries))
            probs = head_probs(mine, keys).astype(jnp.bfloat16)
            part = jnp.dot(probs, values, preferred_element_type=jnp.float32)
            result = part if result is None else jnp.where(lanes, part, result)
        out_ref[0, :, at : at + PAIR] = result.astype(jnp.bfloat16)


def attend_back_kernel(width, qkv_ref, grad_ref, out_ref):
    scale = HEAD ** (-0.5)
    for pair in range(width // PAIR):
        at = pair * PAIR
        queries = qkv_ref[0, :, at : at + PAIR]
        keys = qkv_ref[0, :, width + at : width + at + PAIR]
        values = qkv_ref[0, :, 2 * width + at : 2 * width + at + PAIR]
        grads = grad_ref[0, :, at : at + PAIR]
        grad_q = grad_k = grad_v = 0.0
        for first in (True, False):
            lanes = head_lanes(first)
            zero = jnp.zeros_like(queries)
            my_q = jnp.where(lanes, queries, zero)
            my_k = jnp.where(lanes, keys, zero)
            my_g = jnp.where(lanes, grads, zero)
            probs = head_probs(my_q, keys)
            grad_v = grad_v + matmul_tn(probs.astype(jnp.bfloat16), my_g)
            grad_p = matmul_nt(my_g, values)
            inner = jnp.sum(grad_p * probs, axis=-1, keepdims=True)
            grad_s = (probs * (grad_p - inner)).astype(jnp.bfloat16)
            grad_q = grad_q + jnp.dot(grad_s, my_k, preferred_element_type=jnp.float32)
            grad_k = grad_k + matmul_tn(grad_s, my_q)
        out_ref[0, :, at : at + PAIR] = (grad_q * scale).astype(jnp.bfloat16)
        out_ref[0, :, width + at : width + at + PAIR] = (grad_k * scale).astype(jnp.bfloat16)
        out_ref[0, :, 2 * width + at : 2 * width + at + PAIR] = grad_v.astype(jnp.bfloat16)


def per_image(kernel, columns, n_images, flops, *arrays):
    return pl.pallas_call(
        kernel,
        grid=(n_images,),
        in_specs=[
            pl.BlockSpec((1, SEQ_PAD, array.shape[2]), lambda i: (i, 0, 0)) for array in arrays
        ],
        out_specs=pl.BlockSpec((1, SEQ_PAD, columns), lambda i: (i, 0, 0)),
        out_shape=jax.ShapeDtypeStruct((n_images, SEQ_PAD, columns), jnp.bfloat16),
        compiler_params=pltpu.CompilerParams(vmem_limit_bytes=24 * 1024 * 1024),
        cost_estimate=pl.CostEstimate(
            flops=flops, bytes_accessed=8_000_000, transcendentals=2_000_000
        ),
    )(*arrays)


def pad_rows(values, n_images, fill=0):
    columns = values.shape[1]
    split = values.reshape(n_images, SEQ, columns)
    split = jnp.pad(split, ((0, 0), (0, SEQ_PAD - SEQ), (0, 0)), constant_values=fill)
    return split.reshape(n_images * SEQ_PAD, columns)


def unpad_rows(values, n_images):
    columns = values.shape[1]
    split = values.reshape(n_images, SEQ_PAD, columns)[:, :SEQ]
    return split.reshape(n_images * SEQ, columns)


def pad_columns(parts, multiple):
    total = sum(part.shape[1] for part in parts)
    extra = -total % multiple
    if extra:
        parts = parts + [jnp.zeros((parts[0].shape[0], extra), parts[0].dtype)]
    return jnp.concatenate(parts, axis=1)


SWAP = [(0, 1), (1, 0)]


def sum_replicas(grad):
    low = lax.optimization_barrier(grad.astype(jnp.bfloat16))
    if lax.axis_size("rep") == 2:
        other = lax.ppermute(low, "rep", SWAP)
        return low.astype(jnp.float32) + other.astype(jnp.float32)
    return lax.psum(low, "rep").astype(jnp.float32)


def sum_shared(parts):
    grad = pad_columns(parts, 256)
    rows, columns = grad.shape
    owners = lax.axis_size("exp")
    if lax.axis_size("rep") != 2:
        share = lax.psum_scatter(grad, "exp", scatter_dimension=0, tiled=True)
        return lax.psum(share.astype(jnp.bfloat16), "rep").astype(jnp.float32)
    half = columns // 2
    low = grad.astype(jnp.bfloat16)
    is_first = lax.axis_index("rep") == 0
    left, right = low[:, :half], low[:, half:]
    received = lax.ppermute(jnp.where(is_first, right, left), "rep", SWAP)
    kept = jnp.where(is_first, left, right)
    both = (kept.astype(jnp.float32) + received.astype(jnp.float32)).astype(jnp.bfloat16)
    landed = lax.all_to_all(
        both.reshape(owners, rows // owners, half), "exp", split_axis=0, concat_axis=0, tiled=True
    )
    mine = lax.optimization_barrier(jnp.sum(landed.astype(jnp.float32), axis=0))
    other = lax.ppermute(mine, "rep", SWAP)
    return jnp.concatenate(
        [jnp.where(is_first, mine, other), jnp.where(is_first, other, mine)], axis=1
    )


def on_device(
    tokens,
    ln1_gain,
    ln1_bias,
    qkv_weight,
    out_weight,
    ln2_gain,
    ln2_bias,
    router_weight,
    expert_in,
    expert_out,
    expert_ids,
    slot_ids,
    dropped,
    cotangent,
):
    tok_rows, width = tokens.shape
    n_images = tok_rows // SEQ
    rows = n_images * SEQ_PAD
    local_experts = expert_in.shape[0]
    exp_devices = lax.axis_size("exp")
    num_experts = exp_devices * local_experts
    capacity = (5 * TOP * tok_rows // (4 * num_experts) + 7) // 8 * 8
    slot_total = num_experts * capacity

    def exchange(slots):
        return lax.all_to_all(
            slots.reshape(num_experts, capacity, -1), "exp", split_axis=0, concat_axis=0, tiled=True
        )

    def to_expert(slots):
        arrived = exchange(slots).reshape(exp_devices, local_experts, capacity, -1)
        return arrived.transpose(1, 0, 2, 3).reshape(local_experts, exp_devices * capacity, -1)

    def to_tokens(results):
        outgoing = results.reshape(local_experts, exp_devices, capacity, -1).transpose(1, 0, 2, 3)
        return exchange(outgoing).reshape(slot_total, -1)

    packed = pad_columns(
        [
            qkv_weight,
            out_weight,
            router_weight,
            ln1_gain[:, None],
            ln1_bias[:, None],
            ln2_gain[:, None],
            ln2_bias[:, None],
        ],
        128,
    )
    gathered = lax.all_gather(packed, "exp", axis=0, tiled=True)
    w_qkv = gathered[:, : 3 * width]
    w_attn = gathered[:, 3 * width : 4 * width]
    at = 4 * width + num_experts
    w_router = gathered[:, 4 * width : at]
    norms = gathered[:, at : at + 4].astype(jnp.float32)
    gain_one, bias_one, gain_two, bias_two = (norms[:, i] for i in range(4))

    targets = jnp.where(dropped == 1, slot_total, expert_ids * capacity + slot_ids)
    targets = pad_rows(targets, n_images, slot_total)
    ids = pad_rows(expert_ids, n_images)
    keep_mask = (1 - pad_rows(dropped, n_images)).astype(jnp.float32)
    all_slots = jnp.arange(slot_total, dtype=jnp.int32)[None, :]
    in_slot = [targets[:, k : k + 1] == all_slots for k in range(TOP)]
    pick = [hit.astype(jnp.bfloat16) for hit in in_slot]
    pick_any = (in_slot[0] | in_slot[1]).astype(jnp.bfloat16)

    grad_low = pad_rows(cotangent, n_images)
    grad_slots = matmul_tn(pick_any, grad_low).astype(jnp.bfloat16)
    grad_arrived = to_expert(grad_slots)

    inputs = pad_rows(tokens, n_images).astype(jnp.float32)
    normed1 = layer_norm(inputs, gain_one, bias_one).astype(jnp.bfloat16)
    qkv_low = jnp.dot(normed1, w_qkv, preferred_element_type=jnp.float32).astype(jnp.bfloat16)
    qkv_images = qkv_low.reshape(n_images, SEQ_PAD, 3 * width)
    pair_flops = 2 * n_images * HEADS * SEQ_PAD * SEQ_PAD * PAIR
    attended = per_image(
        functools.partial(attend_kernel, width), width, n_images, 2 * pair_flops, qkv_images
    ).reshape(rows, width)
    mid = inputs + jnp.dot(attended, w_attn, preferred_element_type=jnp.float32)
    normed2 = layer_norm(mid, gain_two, bias_two).astype(jnp.bfloat16)
    expert_rows = to_expert(matmul_tn(pick_any, normed2).astype(jnp.bfloat16))
    logits = jnp.dot(normed2, w_router, preferred_element_type=jnp.float32)
    router_probs = jax.nn.softmax(logits, axis=-1)
    onehot = (
        ids[:, :, None] == jnp.arange(num_experts, dtype=jnp.int32)[None, None, :]
    ).astype(jnp.float32)
    gates = jnp.sum(onehot * router_probs[:, None, :], axis=-1) * keep_mask
    gate_slots = sum(
        jnp.sum(jnp.where(in_slot[k], gates[:, k : k + 1], 0.0), axis=0) for k in range(TOP)
    )
    gates_arrived = to_expert(gate_slots)

    pre_act = jnp.einsum("erd,edf->erf", expert_rows, expert_in, preferred_element_type=jnp.float32)
    hidden, slope = gelu_and_slope(pre_act)
    hidden_low = hidden.astype(jnp.bfloat16)
    slope_low = lax.optimization_barrier(slope.astype(jnp.bfloat16))
    result_low = jnp.einsum(
        "erf,efd->erd", hidden_low, expert_out, preferred_element_type=jnp.float32
    ).astype(jnp.bfloat16)
    returned = to_tokens(result_low)
    grad_result = (gates_arrived * grad_arrived.astype(jnp.float32)).astype(jnp.bfloat16)
    grad_hidden = jnp.einsum(
        "erd,efd->erf", grad_result, expert_out, preferred_element_type=jnp.float32
    )
    grad_pre = (grad_hidden * slope_low.astype(jnp.float32)).astype(jnp.bfloat16)
    grad_sent = jnp.einsum(
        "erf,edf->erd", grad_pre, expert_in, preferred_element_type=jnp.float32
    ).astype(jnp.bfloat16)
    grad_home = to_tokens(grad_sent)
    grad_second = jnp.einsum(
        "erf,erd->efd", hidden_low, grad_result, preferred_element_type=jnp.float32
    )
    grad_first = jnp.einsum(
        "erd,erf->edf", expert_rows, grad_pre, preferred_element_type=jnp.float32
    )
    total_second = sum_replicas(grad_second)
    total_first = sum_replicas(grad_first)

    grad_output = grad_low.astype(jnp.float32)
    back_rows = [jnp.dot(pick[k], returned, preferred_element_type=jnp.float32) for k in range(TOP)]
    moe = sum(gates[:, k : k + 1] * back_rows[k] for k in range(TOP))
    mixed = unpad_rows((mid + moe).astype(jnp.bfloat16), n_images)
    grad_gates = jnp.stack(
        [jnp.sum(grad_output * back_rows[k], axis=-1) for k in range(TOP)], axis=1
    )
    grad_chosen = grad_gates * keep_mask
    grad_probs = jnp.sum(onehot * grad_chosen[:, :, None], axis=1)
    inner_probs = jnp.sum(grad_probs * router_probs, axis=-1, keepdims=True)
    grad_logits = (router_probs * (grad_probs - inner_probs)).astype(jnp.bfloat16)
    grad_router = matmul_tn(normed2, grad_logits)
    grad_normed2 = jnp.dot(pick_any, grad_home, preferred_element_type=jnp.float32)
    grad_normed2 = grad_normed2 + matmul_nt(grad_logits, w_router)
    _, norm_two_pull = jax.vjp(layer_norm, mid, gain_two, bias_two)
    grad_mid_part, grad_gain_two, grad_bias_two = norm_two_pull(grad_normed2)
    grad_mid = grad_output + grad_mid_part
    grad_mid_low = grad_mid.astype(jnp.bfloat16)
    grad_attn_w = matmul_tn(attended, grad_mid_low)
    total_early = sum_shared(
        [grad_attn_w, grad_router, grad_gain_two[:, None], grad_bias_two[:, None]]
    )
    grad_attended = matmul_nt(grad_mid_low, w_attn).astype(jnp.bfloat16)
    grad_qkv_rows = per_image(
        functools.partial(attend_back_kernel, width),
        3 * width,
        n_images,
        5 * pair_flops,
        qkv_images,
        grad_attended.reshape(n_images, SEQ_PAD, width),
    ).reshape(rows, 3 * width)
    grad_qkv_w = matmul_tn(normed1, grad_qkv_rows)
    grad_normed1 = matmul_nt(grad_qkv_rows, w_qkv)
    _, norm_one_pull = jax.vjp(layer_norm, inputs, gain_one, bias_one)
    grad_in_part, grad_gain_one, grad_bias_one = norm_one_pull(grad_normed1)
    grad_tokens = unpad_rows(grad_mid + grad_in_part, n_images)
    total_late = sum_shared([grad_qkv_w, grad_gain_one[:, None], grad_bias_one[:, None]])
    at = width + num_experts
    return (
        mixed,
        grad_tokens,
        total_late[:, 3 * width],
        total_late[:, 3 * width + 1],
        total_late[:, : 3 * width],
        total_early[:, :width],
        total_early[:, at],
        total_early[:, at + 1],
        total_early[:, width:at],
        total_first,
        total_second,
    )


def solution(mesh):
    placed = (
        P(("rep", "exp"), None),
        P("exp"),
        P("exp"),
        P("exp", None),
        P("exp", None),
        P("exp"),
        P("exp"),
        P("exp", None),
        P("exp", None, None),
        P("exp", None, None),
        P(("rep", "exp"), None),
        P(("rep", "exp"), None),
        P(("rep", "exp"), None),
        P(("rep", "exp"), None),
    )
    return jax.shard_map(
        on_device,
        mesh=mesh,
        in_specs=placed,
        out_specs=(
            P(("rep", "exp"), None),
            P(("rep", "exp"), None),
            P("exp"),
            P("exp"),
            P("exp", None),
            P("exp", None),
            P("exp"),
            P("exp"),
            P("exp", None),
            P("exp", None, None),
            P("exp", None, None),
        ),
        check_vma=False,
    )
```

time: 1050 us -> 667 us (0.64)
  waiting for transfers between devices: 377 us -> 264 us
  local copies, waits for them, and re-layouts: 140 us -> 32.4 us
  blocking collectives: 169 us -> 75.4 us
  matrix products: 215 us -> 159 us
  other arithmetic: 96.5 us -> 51.8 us
  Pallas kernels: 0 us -> 24.6 us
  starting transfers between devices: 22.5 us -> 38.8 us
    reduce_scatter x2 -> x0, waiting for transfers between devices: 181 us -> none  [the longest x1 154 us: on_device(): lax.psum_scatter(grad_qkv_w, 'exp', scatter_dimension=0, tiled=True)]
    all_to_all x4 -> x6, waiting for transfers between devices: 52.4 us -> 185 us  [the longest x4 157 us: exchange(): lax.all_to_all(slots.reshape(num_experts, capacity, -1), 'exp', split_axi...]
    all_gather x1 -> x0, blocking collectives: 86.7 us -> none  [on_device(): lax.all_gather(router_weight, 'exp', axis=0, tiled=True)]
    unnamed x2 -> x0, blocking collectives: 78.3 us -> none
    all_to_all x0 -> x1, blocking collectives: none -> 75.4 us  [exchange(): lax.all_to_all(slots.reshape(num_experts, capacity, -1), 'exp', split_axi...]
    unnamed x7 -> x1, waiting for transfers between devices: 59.2 us -> 0.02 us
    reshape x13 -> x8, local copies, waits for them, and re-layouts: 49.3 us -> 5.34 us  [the longest x2 3.06 us: unpad_rows(): return split.reshape(n_images * SEQ, columns)]
    psum x1 -> x0, waiting for transfers between devices: 39.2 us -> none  [on_device(): lax.psum(shares[0].astype(jnp.bfloat16), 'rep').astype(jnp.float32)]
  transfers between devices with their start and end apart: 10 -> 13, of which waited for: 8 -> 8; matrix products, arithmetic and copies ran while one was open for 35% -> 22% of each run, Pallas kernels for 0% -> 3%
where the time goes in v1:
time: 667 us; the launch traced here: 662 us
  waiting for transfers between devices  264 us (40%)
  matrix products  159 us (24%)
  blocking collectives  75.4 us (11%)
  other arithmetic  51.8 us (8%)
  starting transfers between devices  38.8 us (6%)
  local copies, waits for them, and re-layouts  32.4 us (5%)
  Pallas kernels  24.6 us (4%)
  between operations  15.3 us (2%)
    all_to_all x4, waiting for transfers between devices, exchange(): lax.all_to_all(slots.reshape(num_experts, capacity, -1), 'exp', split_axi...  157 us
    all_gather x1, waiting for transfers between devices, on_device(): gathered = lax.all_gather(packed, 'exp', axis=0, tiled=True)  76.9 us
    all_to_all x1, blocking collectives, exchange(): lax.all_to_all(slots.reshape(num_experts, capacity, -1), 'exp', split_axi...  75.4 us
    dot_general x1, matrix products, on_device(): jnp.einsum('erd,edf->erf', expert_rows, expert_in, preferred_element_type...  30 us
    all_to_all x2, waiting for transfers between devices, sum_shared(): lax.all_to_all(both.reshape(owners, rows // owners, half), 'exp', split_a...  28.1 us
    pallas_call x2, Pallas kernels, per_image(): pl.pallas_call(kernel, grid=(n_images,), in_specs=[pl.BlockSpec((1, SEQ_P...  24.6 us
    all_to_all x4, starting transfers between devices, exchange(): lax.all_to_all(slots.reshape(num_experts, capacity, -1), 'exp', split_axi...  21 us
    dot_general x5, matrix products, matmul_tn(): lax.dot_general(left, right, (((0,), (0,)), ((), ())), preferred_element_...  20.4 us
  transfers between devices with their start and end apart: 13, of which 8 were waited for; matrix products, arithmetic and copies ran while one was open for 22% of the time, Pallas kernels for 3%

profile of v1, /device:TPU:13, one launch (start us, length us, event | category | flops | bytes accessed | tf_op | source)
XLA Modules:
  0.0 661.6 jit_solution(9864158681397321585)
XLA Ops:
  18.1 76.9 %all-gather.2.cloned.1.call-done = bf16[768,3200]{1,0:T(8,128)(2,1)} async-done(((bf16[48,3200]{1,0:T(8,128)(2,1)}), bf16[768,3200]{1,0:T(8,128)(2,1)}) %all-gather.2.cloned.1.call-update) | async-done | bytes 4915216 | tf_op jit(solution)/shard_map/all_gather | solution.py:231
  96.9 6.1 convolution_convert_fusion
  103.0 7.6 %shard_map.221 = bf16[4,208,768]{2,1,0:T(8,128)(2,1)S(1)} custom-call(bf16[4,208,2304]{2,1,0:T(8,128)(2,1)S(1)} %bitcast.109), custom_call_target="tpu_custom_call" | custom-call | flops 1063256064 | bytes 8000000 | tf_op jit(solution)/shard_map/pallas_call | solution.py:110
  120.2 75.4 %all_to_all.35 = bf16[16,128,768]{2,1,0:T(8,128)(2,1)S(1)} all-to-all(bf16[16,128,768]{2,1,0:T(8,128)(2,1)S(1)} %bitcast.128), channel_id=1, replica_groups=mesh['rep'=2,'exp'=16] {'exp'}, dimensions={0} | all-to-all | bytes 6291456 | tf_op jit(solution)/shard_map/all_to_all | solution.py:207
  195.6 30.0 %fusion.5 = (bf16[1,2048,3072]{2,1,0:T(8,128)(2,1)}, bf16[2048,3072]{1,0:T(8,128)(2,1)S(1)}) fusion(bf16[2048,768]{1,0:T(8,128)(2,1)S(1)} %bitcast.124, bf16[1,768,3072]{2,1,0:T(8,128)(2,1)S(1)} %bitcast.141), kind=kOutput, calls=%fused_computation.10 | convolution fusion | flops 9833545728 | bytes 33030144 | tf_op jit(solution)/shard_map/erd,edf->erf/dot_general | solution.py:274
  225.6 11.2 %fusion.37 = bf16[2048,768]{1,0:T(8,128)(2,1)} fusion(bf16[2048,3072]{1,0:T(8,128)(2,1)S(1)} %get-tuple-element.102, bf16[1,3072,768]{2,1,0:T(8,128)(2,1)S(1)} %bitcast.139), kind=kOutput, calls=%fused_computation.53 | convolution fusion | flops 9665249280 | bytes 20447232 | tf_op jit(solution)/shard_map/erf,efd->erd/dot_general | solution.py:278
  243.3 6.1 fusion.48
  249.4 62.9 %all-to-all-done.1 = bf16[16,128,768]{2,1,0:T(8,128)(2,1)} async-done(((bf16[16,128,768]{2,1,0:T(8,128)(2,1)}), bf16[16,128,768]{2,1,0:T(8,128)(2,1)}, u32[]{:S(2)}, u32[]{:S(2)}) %all-to-all-start.1) | async-done | bytes 3145760 | tf_op jit(solution)/shard_map/all_to_all | solution.py:207
  324.2 7.4 %fusion.57 = (f32[832]{0:T(1024)S(1)}, f32[832]{0:T(1024)S(1)}, f32[832,768]{1,0:T(8,128)}) fusion(bf16[832,768]{1,0:T(8,128)(2,1)S(1)} %bitcast.117, f32[832,768]{1,0:T(8,128)S(1)} %fusion.6, bf16[2048,768]{1,0:T(8,128)(2,1)} %bitcast.12, s32[832]{0:T(1024)S(1)} %get-tuple-element.97), kind=kOutput, calls=%fused_computation.62 | convolution fusion | flops 2622142976 | bytes 9545472 | tf_op jit(solution)/shard_map/dot_general | solution.py:301
  334.4 52.7 %all-to-all-done.3 = bf16[16,128,768]{2,1,0:T(8,128)(2,1)S(1)} async-done(((bf16[16,128,768]{2,1,0:T(8,128)(2,1)}), bf16[16,128,768]{2,1,0:T(8,128)(2,1)S(1)}, u32[]{:S(2)}, u32[]{:S(2)}) %all-to-all-start.3) | async-done | bytes 3145760 | tf_op jit(solution)/shard_map/all_to_all | solution.py:207
  395.7 16.5 %fusion = bf16[1,2048,3072]{2,1,0:T(8,128)(2,1)} fusion(bf16[1,2048,3072]{2,1,0:T(8,128)(2,1)} %get-tuple-element.101, bf16[1,3072,768]{2,1,0:T(8,128)(2,1)} %param.23, f32[2048]{0:T(1024)S(1)} %bitcast.132, bf16[1,2048,1,1,1,1,768]{6,1,5,4,3,2,0:T(8,128)(2,1)S(1)} %bitcast.115), kind=kOutput, calls=%fused_computation.2 | convolution fusion | flops 9687269376 | bytes 33038336 | tf_op jit(solution)/shard_map/erd,efd->erf/dot_general | solution.py:283
  412.3 15.5 %fusion.40 = bf16[2048,768]{1,0:T(8,128)(2,1)} fusion(bf16[1,768,3072]{2,1,0:T(8,128)(2,1)} %param.22, bf16[1,2048,3072]{2,1,0:T(8,128)(2,1)} %fusion), kind=kOutput, calls=%fused_computation.54 | convolution fusion | flops 9665249280 | bytes 20447232 | tf_op jit(solution)/shard_map/erf,edf->erd/dot_general | solution.py:287
  427.7 6.9 %all-to-all-start.4 = ((bf16[16,128,768]{2,1,0:T(8,128)(2,1)}), bf16[16,128,768]{2,1,0:T(8,128)(2,1)}, u32[]{:S(2)}, u32[]{:S(2)}) async-start(bf16[16,128,768]{2,1,0:T(8,128)(2,1)} %bitcast.127), calls=%async_computation.4 | async-start | bytes 6291456 | tf_op jit(solution)/shard_map/all_to_all | solution.py:207
  437.1 14.8 %fusion.19 = bf16[1,3072,768]{2,1,0:T(8,128)(2,1)} fusion(bf16[2048,3072]{1,0:T(8,128)(2,1)} %copy-done.50, bf16[2048,768]{1,0:T(8,128)(2,1)S(1)} %fusion.9), kind=kOutput, calls=%fused_computation.33 | convolution fusion | flops 9666035712 | bytes 20447232 | tf_op jit(solution)/shard_map/erf,erd->efd/dot_general | solution.py:291
  455.1 12.1 %fusion.20 = bf16[1,768,3072]{2,1,0:T(8,128)(2,1)} fusion(bf16[2048,768]{1,0:T(8,128)(2,1)S(1)} %bitcast.125, bf16[1,2048,3072]{2,1,0:T(8,128)(2,1)S(1)} %bitcast.143), kind=kOutput, calls=%fused_computation.34 | convolution fusion | flops 9666035712 | bytes 20447232 | tf_op jit(solution)/shard_map/erd,erf->edf/dot_general | solution.py:294
  467.4 37.6 %all-to-all-done.4 = bf16[16,128,768]{2,1,0:T(8,128)(2,1)} async-done(((bf16[16,128,768]{2,1,0:T(8,128)(2,1)}), bf16[16,128,768]{2,1,0:T(8,128)(2,1)}, u32[]{:S(2)}, u32[]{:S(2)}) %all-to-all-start.4) | async-done | bytes 3145760 | tf_op jit(solution)/shard_map/all_to_all | solution.py:207
  518.8 17.0 %shard_map.222 = bf16[4,208,2304]{2,1,0:T(8,128)(2,1)S(1)} custom-call(bf16[4,208,2304]{2,1,0:T(8,128)(2,1)S(1)} %bitcast.110, bf16[4,208,768]{2,1,0:T(8,128)(2,1)S(1)} %bitcast.114), custom_call_target="tpu_custom_call" | custom-call | flops 2658140160 | bytes 8000000 | tf_op jit(solution)/shard_map/pallas_call | solution.py:110
  536.0 5.7 multiply_reduce_fusion.1
  543.4 5.7 bitcast_convert_fusion
  549.1 6.7 %concatenate.22 = bf16[768,2560]{1,0:T(8,128)(2,1)} concatenate(bf16[768,2304]{1,0:T(8,128)(2,1)} %bitcast_convert_fusion, bf16[768,1]{1,0:T(8,128)(2,1)} %broadcast_in_dim.105, bf16[768,1]{1,0:T(8,128)(2,1)} %broadcast_in_dim.106, bf16[768,254]{1,0:T(8,128)(2,1)S(1)} %broadcast_in_dim.101), dimensions={1} | concatenate | bytes 7864320 | tf_op jit(solution)/shard_map/concatenate | solution.py:143
  582.8 14.5 %all-to-all-done.6 = bf16[16,48,512]{2,1,0:T(8,128)(2,1)S(1)} async-done(((bf16[16,48,512]{2,1,0:T(8,128)(2,1)}), bf16[16,48,512]{2,1,0:T(8,128)(2,1)S(1)}, u32[]{:S(2)}, u32[]{:S(2)}) %all-to-all-start.6) | async-done | bytes 786464 | tf_op jit(solution)/shard_map/all_to_all | solution.py:171
  602.2 8.6 %convert_add_fusion = f32[1,3072,768]{2,1,0:T(8,128)} fusion(bf16[1,3072,768]{2,1,0:T(8,128)(2,1)} %collective-permute-done.5, bf16[1,3072,768]{2,1,0:T(8,128)(2,1)} %fusion.19), kind=kLoop, calls=%fused_computation.11 | loop fusion | flops 7077888 | bytes 18874368 | tf_op jit(solution)/shard_map/add | solution.py:153
  610.8 9.5 %convert_add_fusion.1 = f32[1,768,3072]{2,1,0:T(8,128)} fusion(bf16[1,768,3072]{2,1,0:T(8,128)(2,1)} %collective-permute-done.4, bf16[1,768,3072]{2,1,0:T(8,128)(2,1)} %fusion.20), kind=kLoop, calls=%fused_computation.12 | loop fusion | flops 7077888 | bytes 18874368 | tf_op jit(solution)/shard_map/add | solution.py:153
  633.9 13.6 %all-to-all-done.5 = bf16[16,48,1280]{2,1,0:T(8,128)(2,1)} async-done(((bf16[16,48,1280]{2,1,0:T(8,128)(2,1)}), bf16[16,48,1280]{2,1,0:T(8,128)(2,1)}, u32[]{:S(2)}, u32[]{:S(2)}) %all-to-all-start.5) | async-done | bytes 1966112 | tf_op jit(solution)/shard_map/all_to_all | solution.py:171
  (236 shorter events, 125.3 us)
Async XLA Ops:
  7.2 87.8 %all-gather.2.cloned.1.call-start = ((), (), s32[]{:S(2)}) async-start(), calls=%async_computation.7 | async-start | bytes 5222400 | tf_op jit(solution)/shard_map/all_gather | solution.py:231
  14.9 82.0 %copy-start.41 = (f32[832]{0:T(1024)}, f32[832]{0:T(1024)S(1)}, u32[]{:S(2)}) copy-start(f32[832]{0:T(1024)S(1)} %div.55) | copy-start | bytes 9988
  16.1 80.7 %copy-start.35 = (f32[832]{0:T(1024)}, f32[832]{0:T(1024)S(1)}, u32[]{:S(2)}) copy-start(f32[832]{0:T(1024)S(1)} %add.144) | copy-start | bytes 9988
  16.1 80.7 %copy-start.43 = (f32[832]{0:T(1024)}, f32[832]{0:T(1024)S(1)}, u32[]{:S(2)}) copy-start(f32[832]{0:T(1024)S(1)} %rsqrt.25) | copy-start | bytes 9988
  96.8 18.3 %copy-start.27 = (f32[768]{0:T(1024)}, f32[768]{0:T(1024)S(1)}, u32[]{:S(2)}) copy-start(f32[768]{0:T(1024)S(1)} %get-tuple-element.85) | copy-start | bytes 9220
  115.1 80.5 %slice-start.4 = ((s8[4718592]{0:T(1024)(128)(4,1)}), s8[4194304]{0:T(1024)(128)(4,1)S(1)}, s32[]{:S(2)}) async-start(s8[4718592]{0:T(1024)(128)(4,1)} %bitcast.140), calls=%async_computation.12 | async-start | bytes 8388608
  115.6 80.0 %slice-start.5 = ((s8[4718592]{0:T(1024)(128)(4,1)}), s8[524288]{0:T(1024)(128)(4,1)S(1)}, s32[]{:S(2)}) async-start(s8[4718592]{0:T(1024)(128)(4,1)} %bitcast.140), calls=%async_computation.13 | async-start | bytes 1048576
  120.2 105.4 %slice-start.2 = ((s8[4718592]{0:T(1024)(128)(4,1)}), s8[4194304]{0:T(1024)(128)(4,1)S(1)}, s32[]{:S(2)}) async-start(s8[4718592]{0:T(1024)(128)(4,1)} %bitcast.138), calls=%async_computation.10 | async-start | bytes 8388608
  195.6 30.0 %copy-start.16 = (bf16[16,128,768]{2,1,0:T(8,128)(2,1)}, bf16[16,128,768]{2,1,0:T(8,128)(2,1)S(1)}, u32[]{:S(2)}) copy-start(bf16[16,128,768]{2,1,0:T(8,128)(2,1)S(1)} %all_to_all.35) | copy-start | bytes 9437188
  195.6 30.0 %slice-start.3 = ((s8[4718592]{0:T(1024)(128)(4,1)}), s8[524288]{0:T(1024)(128)(4,1)S(1)}, s32[]{:S(2)}) async-start(s8[4718592]{0:T(1024)(128)(4,1)} %bitcast.138), calls=%async_computation.11 | async-start | bytes 1048576
  236.8 75.5 %all-to-all-start.1 = ((bf16[16,128,768]{2,1,0:T(8,128)(2,1)}), bf16[16,128,768]{2,1,0:T(8,128)(2,1)}, u32[]{:S(2)}, u32[]{:S(2)}) async-start(bf16[16,128,768]{2,1,0:T(8,128)(2,1)} %bitcast.11), calls=%async_computation.1 | async-start | bytes 6291456 | tf_op jit(solution)/shard_map/all_to_all | solution.py:207
  312.3 74.8 %all-to-all-start.3 = ((bf16[16,128,768]{2,1,0:T(8,128)(2,1)}), bf16[16,128,768]{2,1,0:T(8,128)(2,1)S(1)}, u32[]{:S(2)}, u32[]{:S(2)}) async-start(bf16[16,128,768]{2,1,0:T(8,128)(2,1)} %bitcast.126), calls=%async_computation.3 | async-start | bytes 6291456 | tf_op jit(solution)/shard_map/all_to_all | solution.py:207
  387.1 8.6 %all-to-all-start.2 = ((f32[16,128,1]{1,2,0:T(1,128)}), f32[16,128,1]{1,2,0:T(1,128)S(1)}, u32[]{:S(2)}, u32[]{:S(2)}) async-start(f32[16,128,1]{1,2,0:T(1,128)} %bitcast.16), calls=%async_computation.2 | async-start | bytes 16384 | tf_op jit(solution)/shard_map/all_to_all | solution.py:207
  427.7 77.2 %all-to-all-start.4 = ((bf16[16,128,768]{2,1,0:T(8,128)(2,1)}), bf16[16,128,768]{2,1,0:T(8,128)(2,1)}, u32[]{:S(2)}, u32[]{:S(2)}) async-start(bf16[16,128,768]{2,1,0:T(8,128)(2,1)} %bitcast.127), calls=%async_computation.4 | async-start | bytes 6291456 | tf_op jit(solution)/shard_map/all_to_all | solution.py:207
  436.5 18.6 %slice-start.6 = ((s8[12582912]{0:T(1024)(128)(4,1)}), s8[4194304]{0:T(1024)(128)(4,1)S(1)}, s32[]{:S(2)}) async-start(s8[12582912]{0:T(1024)(128)(4,1)} %bitcast.142), calls=%async_computation.14 | async-start | bytes 8388608
  437.1 18.0 %copy-start.17 = (bf16[16,128,768]{2,1,0:T(8,128)(2,1)S(1)}, bf16[16,128,768]{2,1,0:T(8,128)(2,1)}, u32[]{:S(2)}) copy-start(bf16[16,128,768]{2,1,0:T(8,128)(2,1)} %copy-done.16) | copy-start | bytes 9437188
  452.0 150.2 %collective-permute-start.5 = (bf16[1,3072,768]{2,1,0:T(8,128)(2,1)}, bf16[1,3072,768]{2,1,0:T(8,128)(2,1)}, u32[]{:S(2)}, u32[]{:S(2)}) collective-permute-start(bf16[1,3072,768]{2,1,0:T(8,128)(2,1)} %fusion.19), channel_id=1, source_target_pairs={{0,16},{16,0},{1,17},{17,1},{2,18},{18,2},{3,19},{19,3},{4,20},{20... | collective-permute-start | bytes 14155784 | tf_op jit(solution)/shard_map/ppermute | solution.py:152
  467.3 143.5 %collective-permute-start.4 = (bf16[1,768,3072]{2,1,0:T(8,128)(2,1)}, bf16[1,768,3072]{2,1,0:T(8,128)(2,1)}, u32[]{:S(2)}, u32[]{:S(2)}) collective-permute-start(bf16[1,768,3072]{2,1,0:T(8,128)(2,1)} %fusion.20), channel_id=1, source_target_pairs={{0,16},{16,0},{1,17},{17,1},{2,18},{18,2},{3,19},{19,3},{4,20},{20... | collective-permute-start | bytes 14155784 | tf_op jit(solution)/shard_map/ppermute | solution.py:152
  559.6 18.4 %collective-permute-start = (bf16[768,1280]{1,0:T(8,128)(2,1)}, bf16[768,1280]{1,0:T(8,128)(2,1)}, u32[]{:S(2)}, u32[]{:S(2)}) collective-permute-start(bf16[768,1280]{1,0:T(8,128)(2,1)} %broadcast_select_fusion), channel_id=1, source_target_pairs={{0,16},{16,0},{1,17},{17,1},{2,18},{18,2},{3,19},{19,3},{4,20},{20... | collective-permute-start | bytes 5898248 | tf_op jit(solution)/shard_map/ppermute | solution.py:168
  569.0 2.4 collective-permute-start.2
  573.7 23.6 %all-to-all-start.6 = ((bf16[16,48,512]{2,1,0:T(8,128)(2,1)}), bf16[16,48,512]{2,1,0:T(8,128)(2,1)S(1)}, u32[]{:S(2)}, u32[]{:S(2)}) async-start(bf16[16,48,512]{2,1,0:T(8,128)(2,1)} %bitcast.129), calls=%async_computation.6 | async-start | bytes 1572864 | tf_op jit(solution)/shard_map/all_to_all | solution.py:171
  597.3 50.3 %all-to-all-start.5 = ((bf16[16,48,1280]{2,1,0:T(8,128)(2,1)}), bf16[16,48,1280]{2,1,0:T(8,128)(2,1)}, u32[]{:S(2)}, u32[]{:S(2)}) async-start(bf16[16,48,1280]{2,1,0:T(8,128)(2,1)} %bitcast.122), calls=%async_computation.5 | async-start | bytes 3932160 | tf_op jit(solution)/shard_map/all_to_all | solution.py:171
  631.7 19.2 %collective-permute-start.3 = (f32[48,512]{1,0:T(8,128)S(1)}, f32[48,512]{1,0:T(8,128)S(1)}, u32[]{:S(2)}, u32[]{:S(2)}) collective-permute-start(f32[48,512]{1,0:T(8,128)S(1)} %convert_reduce_fusion.2), channel_id=1, source_target_pairs={{0,16},{16,0},{1,17},{17,1},{2,18},{18,2},{3,19},{19,3},{4,20},{20... | collective-permute-start | bytes 294920 | tf_op jit(solution)/shard_map/ppermute | solution.py:175
  649.4 3.6 collective-permute-start.1
  (49 other events, 325.1 us)
Sparse Core Ops, SparseCore 0:
  13.0 81.9 all-gather.1

commit v2 on v1

--- a/solution.py
+++ b/solution.py
@@ -154,28 +154,48 @@
     return lax.psum(low, "rep").astype(jnp.float32)
 
 
-def sum_shared(parts):
-    grad = pad_columns(parts, 256)
-    rows, columns = grad.shape
+def start_shared(left, right, small):
+    small = pad_columns(small, 128).astype(jnp.bfloat16)
+    if lax.axis_size("rep") != 2:
+        grad = jnp.concatenate([matmul_tn(left, right), small.astype(jnp.float32)], axis=1)
+        return lax.psum_scatter(grad, "exp", scatter_dimension=0, tiled=True)
+    half = right.shape[1] // 2
+    place = lax.axis_index("rep")
+
+    def product(which):
+        columns = lax.dynamic_slice_in_dim(right, which * half, half, axis=1)
+        return matmul_tn(left, columns).astype(jnp.bfloat16)
+
+    received = lax.ppermute(product(1 - place), "rep", SWAP)
+    small = lax.optimization_barrier(small)
+    small_received = lax.ppermute(small, "rep", SWAP)
+    both = product(place).astype(jnp.float32) + received.astype(jnp.float32)
+    small_both = small.astype(jnp.float32) + small_received.astype(jnp.float32)
+    return jnp.concatenate([both.astype(jnp.bfloat16), small_both.astype(jnp.bfloat16)], axis=1)
+
+
+def send_shared(both):
+    if lax.axis_size("rep") != 2:
+        return both
     owners = lax.axis_size("exp")
+    parts = both.reshape(owners, both.shape[0] // owners, both.shape[1])
+    return lax.all_to_all(parts, "exp", split_axis=0, concat_axis=0, tiled=True)
+
+
+def finish_shared(landed, columns):
     if lax.axis_size("rep") != 2:
-        share = lax.psum_scatter(grad, "exp", scatter_dimension=0, tiled=True)
-        return lax.psum(share.astype(jnp.bfloat16), "rep").astype(jnp.float32)
+        total = lax.psum(landed.astype(jnp.bfloat16), "rep").astype(jnp.float32)
+        return total[:, :columns], total[:, columns:]
     half = columns // 2
-    low = grad.astype(jnp.bfloat16)
     is_first = lax.axis_index("rep") == 0
-    left, right = low[:, :half], low[:, half:]
-    received = lax.ppermute(jnp.where(is_first, right, left), "rep", SWAP)
-    kept = jnp.where(is_first, left, right)
-    both = (kept.astype(jnp.float32) + received.astype(jnp.float32)).astype(jnp.bfloat16)
-    landed = lax.all_to_all(
-        both.reshape(owners, rows // owners, half), "exp", split_axis=0, concat_axis=0, tiled=True
-    )
     mine = lax.optimization_barrier(jnp.sum(landed.astype(jnp.float32), axis=0))
+    small = mine[:, half:]
+    mine = mine[:, :half]
     other = lax.ppermute(mine, "rep", SWAP)
-    return jnp.concatenate(
+    large = jnp.concatenate(
         [jnp.where(is_first, mine, other), jnp.where(is_first, other, mine)], axis=1
     )
+    return large, small
 
 
 def on_device(
@@ -221,21 +241,11 @@
             qkv_weight,
             out_weight,
             router_weight,
-            ln1_gain[:, None],
-            ln1_bias[:, None],
-            ln2_gain[:, None],
-            ln2_bias[:, None],
+            jnp.stack([ln1_gain, ln1_bias, ln2_gain, ln2_bias], axis=1),
         ],
         128,
     )
     gathered = lax.all_gather(packed, "exp", axis=0, tiled=True)
-    w_qkv = gathered[:, : 3 * width]
-    w_attn = gathered[:, 3 * width : 4 * width]
-    at = 4 * width + num_experts
-    w_router = gathered[:, 4 * width : at]
-    norms = gathered[:, at : at + 4].astype(jnp.float32)
-    gain_one, bias_one, gain_two, bias_two = (norms[:, i] for i in range(4))
-
     targets = jnp.where(dropped == 1, slot_total, expert_ids * capacity + slot_ids)
     targets = pad_rows(targets, n_images, slot_total)
     ids = pad_rows(expert_ids, n_images)
@@ -244,18 +254,23 @@
     in_slot = [targets[:, k : k + 1] == all_slots for k in range(TOP)]
     pick = [hit.astype(jnp.bfloat16) for hit in in_slot]
     pick_any = (in_slot[0] | in_slot[1]).astype(jnp.bfloat16)
-
     grad_low = pad_rows(cotangent, n_images)
     grad_slots = matmul_tn(pick_any, grad_low).astype(jnp.bfloat16)
-    grad_arrived = to_expert(grad_slots)
+    gathered, grad_arrived = lax.optimization_barrier((gathered, to_expert(grad_slots)))
+
+    w_qkv = gathered[:, : 3 * width]
+    w_attn = gathered[:, 3 * width : 4 * width]
+    at = 4 * width + num_experts
+    w_router = gathered[:, 4 * width : at]
+    norms = gathered[:, at : at + 4].astype(jnp.float32)
+    gain_one, bias_one, gain_two, bias_two = (norms[:, i] for i in range(4))
 
     inputs = pad_rows(tokens, n_images).astype(jnp.float32)
     normed1 = layer_norm(inputs, gain_one, bias_one).astype(jnp.bfloat16)
     qkv_low = jnp.dot(normed1, w_qkv, preferred_element_type=jnp.float32).astype(jnp.bfloat16)
     qkv_images = qkv_low.reshape(n_images, SEQ_PAD, 3 * width)
-    pair_flops = 2 * n_images * HEADS * SEQ_PAD * SEQ_PAD * PAIR
     attended = per_image(
-        functools.partial(attend_kernel, width), width, n_images, 2 * pair_flops, qkv_images
+        functools.partial(attend_kernel, width), width, n_images, 8_000_000_000, qkv_images
     ).reshape(rows, width)
     mid = inputs + jnp.dot(attended, w_attn, preferred_element_type=jnp.float32)
     normed2 = layer_norm(mid, gain_two, bias_two).astype(jnp.bfloat16)
@@ -266,10 +281,13 @@
         ids[:, :, None] == jnp.arange(num_experts, dtype=jnp.int32)[None, None, :]
     ).astype(jnp.float32)
     gates = jnp.sum(onehot * router_probs[:, None, :], axis=-1) * keep_mask
-    gate_slots = sum(
-        jnp.sum(jnp.where(in_slot[k], gates[:, k : k + 1], 0.0), axis=0) for k in range(TOP)
-    )
-    gates_arrived = to_expert(gate_slots)
+    own = lax.axis_index("exp") * local_experts + jnp.arange(local_experts, dtype=jnp.int32)
+    own_column = own[:, None, None] == jnp.arange(num_experts, dtype=jnp.int32)[None, None, :]
+    slot_probs = jax.nn.softmax(
+        jnp.einsum("erd,dn->ern", expert_rows, w_router, preferred_element_type=jnp.float32),
+        axis=-1,
+    )
+    gates_arrived = jnp.sum(jnp.where(own_column, slot_probs, 0.0), axis=-1, keepdims=True)
 
     pre_act = jnp.einsum("erd,edf->erf", expert_rows, expert_in, preferred_element_type=jnp.float32)
     hidden, slope = gelu_and_slope(pre_act)
@@ -315,36 +333,42 @@
     grad_mid_part, grad_gain_two, grad_bias_two = norm_two_pull(grad_normed2)
     grad_mid = grad_output + grad_mid_part
     grad_mid_low = grad_mid.astype(jnp.bfloat16)
-    grad_attn_w = matmul_tn(attended, grad_mid_low)
-    total_early = sum_shared(
-        [grad_attn_w, grad_router, grad_gain_two[:, None], grad_bias_two[:, None]]
+    early = start_shared(
+        attended,
+        grad_mid_low,
+        [grad_router, jnp.stack([grad_gain_two, grad_bias_two], axis=1)],
     )
     grad_attended = matmul_nt(grad_mid_low, w_attn).astype(jnp.bfloat16)
+    early, grad_attended = lax.optimization_barrier((early, grad_attended))
+    early_landed = send_shared(early)
     grad_qkv_rows = per_image(
         functools.partial(attend_back_kernel, width),
         3 * width,
         n_images,
-        5 * pair_flops,
+        20_000_000_000,
         qkv_images,
         grad_attended.reshape(n_images, SEQ_PAD, width),
     ).reshape(rows, 3 * width)
-    grad_qkv_w = matmul_tn(normed1, grad_qkv_rows)
+    early_landed, grad_qkv_rows = lax.optimization_barrier((early_landed, grad_qkv_rows))
+    out_total, early_small = finish_shared(early_landed, width)
     grad_normed1 = matmul_nt(grad_qkv_rows, w_qkv)
     _, norm_one_pull = jax.vjp(layer_norm, inputs, gain_one, bias_one)
     grad_in_part, grad_gain_one, grad_bias_one = norm_one_pull(grad_normed1)
     grad_tokens = unpad_rows(grad_mid + grad_in_part, n_images)
-    total_late = sum_shared([grad_qkv_w, grad_gain_one[:, None], grad_bias_one[:, None]])
-    at = width + num_experts
+    late = start_shared(
+        normed1, grad_qkv_rows, [jnp.stack([grad_gain_one, grad_bias_one], axis=1)]
+    )
+    qkv_total, late_small = finish_shared(send_shared(late), 3 * width)
     return (
         mixed,
         grad_tokens,
-        total_late[:, 3 * width],
-        total_late[:, 3 * width + 1],
-        total_late[:, : 3 * width],
-        total_early[:, :width],
-        total_early[:, at],
-        total_early[:, at + 1],
-        total_early[:, width:at],
+        late_small[:, 0],
+        late_small[:, 1],
+        qkv_total,
+        out_total,
+        early_small[:, num_experts],
+        early_small[:, num_experts + 1],
+        early_small[:, :num_experts],
         total_first,
         total_second,
     )

time: 667 us -> 602 us (0.903)
  blocking collectives: 75.4 us -> 0 us
  matrix products: 159 us -> 173 us
  waiting for transfers between devices: 264 us -> 278 us
  other arithmetic: 51.8 us -> 39.6 us
    all_to_all x4, waiting for transfers between devices: 157 us -> 256 us  [exchange(): lax.all_to_all(slots.reshape(num_experts, capacity, -1), 'exp', split_axi...]
    all_to_all x1 -> x0, blocking collectives: 75.4 us -> none  [exchange(): lax.all_to_all(slots.reshape(num_experts, capacity, -1), 'exp', split_axi...]
    all_gather x1, waiting for transfers between devices: 76.9 us -> 9.66 us  [on_device(): gathered = lax.all_gather(packed, 'exp', axis=0, tiled=True)]
    all_to_all x2, waiting for transfers between devices: 28.1 us -> 10.7 us  [send_shared(): return lax.all_to_all(parts, 'exp', split_axis=0, concat_axis=0, tiled=True)]
    concatenate x3, local copies, waits for them, and re-layouts: 12.3 us -> 1.96 us  [pad_columns(): return jnp.concatenate(parts, axis=1)]
    convert_element_type x3, other arithmetic: 7.67 us -> 0.56 us  [the longest x1 0.46 us: on_device(): normed1 = layer_norm(inputs, gain_one, bias_one).astype(jnp.bfloat16)]
    dot_general x5 -> x7, matrix products: 20.4 us -> 23.4 us  [matmul_tn(): lax.dot_general(left, right, (((0,), (0,)), ((), ())), preferred_element_...]
  transfers between devices with their start and end apart: 13 -> 15, of which waited for: 8 -> 7; matrix products, arithmetic and copies ran while one was open for 22% -> 23% of each run, Pallas kernels for 3% -> 3%
where the time goes in v2:
time: 602 us; the launch traced here: 598 us
  waiting for transfers between devices  278 us (46%)
  matrix products  173 us (29%)
  starting transfers between devices  41.4 us (7%)
  other arithmetic  39.6 us (7%)
  local copies, waits for them, and re-layouts  27.1 us (5%)
  Pallas kernels  23.9 us (4%)
  between operations  15.2 us (3%)
    all_to_all x4, waiting for transfers between devices, exchange(): lax.all_to_all(slots.reshape(num_experts, capacity, -1), 'exp', split_axi...  256 us
    dot_general x1, matrix products, on_device(): jnp.einsum('erd,edf->erf', expert_rows, expert_in, preferred_element_type...  32.7 us
    pallas_call x2, Pallas kernels, per_image(): pl.pallas_call(kernel, grid=(n_images,), in_specs=[pl.BlockSpec((1, SEQ_P...  23.9 us
    all_to_all x4, starting transfers between devices, exchange(): lax.all_to_all(slots.reshape(num_experts, capacity, -1), 'exp', split_axi...  23.4 us
    dot_general x7, matrix products, matmul_tn(): lax.dot_general(left, right, (((0,), (0,)), ((), ())), preferred_element_...  23.4 us
    add x2, other arithmetic, sum_replicas(): return low.astype(jnp.float32) + other.astype(jnp.float32)  18 us
    dot_general x1, matrix products, on_device(): jnp.einsum('erd,efd->erf', grad_result, expert_out, preferred_element_typ...  17.5 us
    dot_general x1, matrix products, on_device(): jnp.einsum('erf,erd->efd', hidden_low, grad_result, preferred_element_typ...  16.3 us
  transfers between devices with their start and end apart: 15, of which 7 were waited for; matrix products, arithmetic and copies ran while one was open for 23% of the time, Pallas kernels for 3%

profile of v2, /device:TPU:13, one launch (start us, length us, event | category | flops | bytes accessed | tf_op | source)
XLA Modules:
  0.0 597.7 jit_solution(10731362215195212)
XLA Ops:
  14.9 6.0 %fusion.44 = bf16[2048,768]{1,0:T(8,128)(2,1)} fusion(bf16[832,768]{1,0:T(8,128)(2,1)S(1)} %bitcast.116, s32[832]{0:T(1024)S(1)} %get-tuple-element.99, s32[832]{0:T(1024)S(1)} %get-tuple-element.98), kind=kOutput, calls=%fused_computation.50 | convolution fusion | flops 2623930368 | bytes 4430336 | tf_op jit(solution)/shard_map/dot_general | solution.py:42
  20.9 7.1 %all-to-all-start = ((bf16[16,128,768]{2,1,0:T(8,128)(2,1)}), bf16[16,128,768]{2,1,0:T(8,128)(2,1)}, u32[]{:S(2)}, u32[]{:S(2)}) async-start(bf16[16,128,768]{2,1,0:T(8,128)(2,1)} %bitcast.121), calls=%async_computation | async-start | bytes 6291456 | tf_op jit(solution)/shard_map/all_to_all | solution.py:227
  31.5 100.9 %all-to-all-done = bf16[16,128,768]{2,1,0:T(8,128)(2,1)} async-done(((bf16[16,128,768]{2,1,0:T(8,128)(2,1)}), bf16[16,128,768]{2,1,0:T(8,128)(2,1)}, u32[]{:S(2)}, u32[]{:S(2)}) %all-to-all-start) | async-done | bytes 3145760 | tf_op jit(solution)/shard_map/all_to_all | solution.py:227
  132.3 9.7 %all-gather.2.cloned.1.call-done = bf16[768,3200]{1,0:T(8,128)(2,1)} async-done(((bf16[48,3200]{1,0:T(8,128)(2,1)}), bf16[768,3200]{1,0:T(8,128)(2,1)}) %all-gather.2.cloned.1.call-update) | async-done | bytes 4915216 | tf_op jit(solution)/shard_map/all_gather | solution.py:248
  148.8 7.1 %shard_map.221 = bf16[4,208,768]{2,1,0:T(8,128)(2,1)S(1)} custom-call(bf16[4,208,2304]{2,1,0:T(8,128)(2,1)S(1)} %bitcast.102), custom_call_target="tpu_custom_call" | custom-call | flops 8000000000 | bytes 8000000 | tf_op jit(solution)/shard_map/pallas_call | solution.py:110
  159.2 6.1 %fusion.47 = bf16[2048,768]{1,0:T(8,128)(2,1)} fusion(bf16[832,768]{1,0:T(8,128)(2,1)S(1)} %add_convert_fusion.3, s32[832]{0:T(1024)S(1)} %get-tuple-element.99, s32[832]{0:T(1024)S(1)} %get-tuple-element.98), kind=kOutput, calls=%fused_computation.51 | convolution fusion | flops 2623930368 | bytes 4430336 | tf_op jit(solution)/shard_map/dot_general | solution.py:42
  165.3 6.8 %all-to-all-start.1 = ((bf16[16,128,768]{2,1,0:T(8,128)(2,1)}), bf16[16,128,768]{2,1,0:T(8,128)(2,1)S(1)}, u32[]{:S(2)}, u32[]{:S(2)}) async-start(bf16[16,128,768]{2,1,0:T(8,128)(2,1)} %bitcast.122), calls=%async_computation.1 | async-start | bytes 6291456 | tf_op jit(solution)/shard_map/all_to_all | solution.py:227
  172.1 70.4 %all-to-all-done.1 = bf16[16,128,768]{2,1,0:T(8,128)(2,1)S(1)} async-done(((bf16[16,128,768]{2,1,0:T(8,128)(2,1)}), bf16[16,128,768]{2,1,0:T(8,128)(2,1)S(1)}, u32[]{:S(2)}, u32[]{:S(2)}) %all-to-all-start.1) | async-done | bytes 3145760 | tf_op jit(solution)/shard_map/all_to_all | solution.py:227
  244.3 32.7 %fusion.5 = (bf16[1,2048,3072]{2,1,0:T(8,128)(2,1)}, bf16[2048,3072]{1,0:T(8,128)(2,1)}) fusion(bf16[2048,768]{1,0:T(8,128)(2,1)S(1)} %bitcast.114, bf16[1,768,3072]{2,1,0:T(8,128)(2,1)} %param.22), kind=kOutput, calls=%fused_computation.10 | convolution fusion | flops 9833545728 | bytes 33030144 | tf_op jit(solution)/shard_map/erd,edf->erf/dot_general | solution.py:292
  277.2 17.5 %fusion = bf16[1,2048,3072]{2,1,0:T(8,128)(2,1)} fusion(bf16[1,2048,3072]{2,1,0:T(8,128)(2,1)} %get-tuple-element.102, bf16[1,3072,768]{2,1,0:T(8,128)(2,1)} %param.23, bf16[1,2048,768]{2,1,0:T(8,128)(2,1)} %bitcast.7, f32[2048]{0:T(1024)S(1)} %select_reduce_fusion), kind=kOutput, calls=%fused_computation.2 | convolution fusion | flops 9687269376 | bytes 33038336 | tf_op jit(solution)/shard_map/erd,efd->erf/dot_general | solution.py:301
  294.6 15.9 %fusion.39 = bf16[2048,768]{1,0:T(8,128)(2,1)} fusion(bf16[1,768,3072]{2,1,0:T(8,128)(2,1)} %param.22, bf16[1,2048,3072]{2,1,0:T(8,128)(2,1)} %fusion), kind=kOutput, calls=%fused_computation.49 | convolution fusion | flops 9665249280 | bytes 20447232 | tf_op jit(solution)/shard_map/erf,edf->erd/dot_general | solution.py:305
  315.3 15.4 %fusion.36 = bf16[2048,768]{1,0:T(8,128)(2,1)} fusion(bf16[2048,3072]{1,0:T(8,128)(2,1)} %get-tuple-element.103, bf16[1,3072,768]{2,1,0:T(8,128)(2,1)} %param.23), kind=kOutput, calls=%fused_computation.48 | convolution fusion | flops 9665249280 | bytes 20447232 | tf_op jit(solution)/shard_map/erf,efd->erd/dot_general | solution.py:296
  330.7 55.1 %all-to-all-done.3 = bf16[16,128,768]{2,1,0:T(8,128)(2,1)} async-done(((bf16[16,128,768]{2,1,0:T(8,128)(2,1)}), bf16[16,128,768]{2,1,0:T(8,128)(2,1)}, u32[]{:S(2)}, u32[]{:S(2)}) %all-to-all-start.3) | async-done | bytes 3145760 | tf_op jit(solution)/shard_map/all_to_all | solution.py:227
  392.8 14.4 %fusion.19 = bf16[1,768,3072]{2,1,0:T(8,128)(2,1)} fusion(bf16[2048,768]{1,0:T(8,128)(2,1)S(1)} %bitcast.115, bf16[1,2048,3072]{2,1,0:T(8,128)(2,1)} %fusion), kind=kOutput, calls=%fused_computation.29 | convolution fusion | flops 9666035712 | bytes 20447232 | tf_op jit(solution)/shard_map/erd,erf->edf/dot_general | solution.py:312
  409.3 16.3 %fusion.18 = bf16[1,3072,768]{2,1,0:T(8,128)(2,1)} fusion(bf16[2048,3072]{1,0:T(8,128)(2,1)} %get-tuple-element.103, bf16[1,2048,768]{2,1,0:T(8,128)(2,1)} %bitcast.7, f32[2048]{0:T(1024)S(1)} %select_reduce_fusion), kind=kOutput, calls=%fused_computation.28 | convolution fusion | flops 9670754304 | bytes 20455424 | tf_op jit(solution)/shard_map/erf,erd->efd/dot_general | solution.py:309
  425.6 5.4 fusion.22
  431.1 29.7 %all-to-all-done.2 = bf16[16,128,768]{2,1,0:T(8,128)(2,1)} async-done(((bf16[16,128,768]{2,1,0:T(8,128)(2,1)}), bf16[16,128,768]{2,1,0:T(8,128)(2,1)}, u32[]{:S(2)}, u32[]{:S(2)}) %all-to-all-start.2) | async-done | bytes 3145760 | tf_op jit(solution)/shard_map/all_to_all | solution.py:227
  465.9 5.3 fusion.54
  492.2 16.8 %shard_map.222 = bf16[4,208,2304]{2,1,0:T(8,128)(2,1)S(1)} custom-call(bf16[4,208,2304]{2,1,0:T(8,128)(2,1)S(1)} %bitcast.103, bf16[4,208,768]{2,1,0:T(8,128)(2,1)S(1)} %bitcast.110), custom_call_target="tpu_custom_call" | custom-call | flops 20000000000 | bytes 8000000 | tf_op jit(solution)/shard_map/pallas_call | solution.py:110
  517.2 8.5 %multiply_reduce_fusion = (bf16[768]{0:T(1024)(128)(2,1)S(1)}, f32[832]{0:T(1024)S(1)}, bf16[768]{0:T(1024)(128)(2,1)S(1)}, f32[832,768]{1,0:T(8,128)}) fusion(f32[832]{0:T(1024)S(1)} %copy-done.39, f32[832]{0:T(1024)S(1)} %copy-done.37, f32[4,208,768]{2,1,0:T(8,128)} %copy-done.10, f32[768]{0:T(1024)S(1)} %copy-done.35, f32[832,768]{1,0:T(8,128)} %bitcast.112, ...), kind=kOutput, calls=%fused_computation.60 | convolution fusion | flops 2950149888 | bytes 15056640 | tf_op jit(solution)/shard_map/dot_general | solution.py:48
  533.4 6.7 %all-to-all-start.5 = ((bf16[16,48,1280]{2,1,0:T(8,128)(2,1)}), bf16[16,48,1280]{2,1,0:T(8,128)(2,1)}, u32[]{:S(2)}, u32[]{:S(2)}) async-start(bf16[16,48,1280]{2,1,0:T(8,128)(2,1)} %bitcast.27), calls=%async_computation.5 | async-start | bytes 3932160 | tf_op jit(solution)/shard_map/all_to_all | solution.py:182
  540.1 9.4 %convert_add_fusion.1 = f32[1,768,3072]{2,1,0:T(8,128)} fusion(bf16[1,768,3072]{2,1,0:T(8,128)(2,1)} %collective-permute-done.6, bf16[1,768,3072]{2,1,0:T(8,128)(2,1)} %fusion.19), kind=kLoop, calls=%fused_computation.12 | loop fusion | flops 7077888 | bytes 18874368 | tf_op jit(solution)/shard_map/add | solution.py:153
  549.5 8.6 %convert_add_fusion = f32[1,3072,768]{2,1,0:T(8,128)} fusion(bf16[1,3072,768]{2,1,0:T(8,128)(2,1)} %collective-permute-done.7, bf16[1,3072,768]{2,1,0:T(8,128)(2,1)} %fusion.18), kind=kLoop, calls=%fused_computation.11 | loop fusion | flops 7077888 | bytes 18874368 | tf_op jit(solution)/shard_map/add | solution.py:153
  574.5 10.7 %all-to-all-done.5 = bf16[16,48,1280]{2,1,0:T(8,128)(2,1)} async-done(((bf16[16,48,1280]{2,1,0:T(8,128)(2,1)}), bf16[16,48,1280]{2,1,0:T(8,128)(2,1)}, u32[]{:S(2)}, u32[]{:S(2)}) %all-to-all-start.5) | async-done | bytes 1966112 | tf_op jit(solution)/shard_map/all_to_all | solution.py:182
  (221 shorter events, 100.2 us)
Async XLA Ops:
  7.2 134.8 %all-gather.2.cloned.1.call-start = ((), (), s32[]{:S(2)}) async-start(), calls=%async_computation.6 | async-start | bytes 5222400 | tf_op jit(solution)/shard_map/all_gather | solution.py:248
  14.9 144.3 %copy-start.45 = (s32[832]{0:T(1024)}, s32[832]{0:T(1024)S(1)}, u32[]{:S(2)}) copy-start(s32[832]{0:T(1024)S(1)} %get-tuple-element.98) | copy-start | bytes 9988
  14.9 144.3 %copy-start.47 = (s32[832]{0:T(1024)}, s32[832]{0:T(1024)S(1)}, u32[]{:S(2)}) copy-start(s32[832]{0:T(1024)S(1)} %get-tuple-element.99) | copy-start | bytes 9988
  20.9 111.5 %all-to-all-start = ((bf16[16,128,768]{2,1,0:T(8,128)(2,1)}), bf16[16,128,768]{2,1,0:T(8,128)(2,1)}, u32[]{:S(2)}, u32[]{:S(2)}) async-start(bf16[16,128,768]{2,1,0:T(8,128)(2,1)} %bitcast.121), calls=%async_computation | async-start | bytes 6291456 | tf_op jit(solution)/shard_map/all_to_all | solution.py:227
  28.7 115.2 %copy-start.36 = (f32[832]{0:T(1024)}, f32[832]{0:T(1024)S(1)}, u32[]{:S(2)}) copy-start(f32[832]{0:T(1024)S(1)} %div.64) | copy-start | bytes 9988
  30.0 114.0 %copy-start.38 = (f32[832]{0:T(1024)}, f32[832]{0:T(1024)S(1)}, u32[]{:S(2)}) copy-start(f32[832]{0:T(1024)S(1)} %rsqrt.22) | copy-start | bytes 9988
  31.5 124.5 %copy-start.10 = (f32[4,208,768]{2,1,0:T(8,128)}, f32[4,208,768]{2,1,0:T(8,128)S(1)}, u32[]{:S(2)}) copy-start(f32[4,208,768]{2,1,0:T(8,128)S(1)} %pad_convert_fusion) | copy-start | bytes 7667716
  143.9 14.8 %copy-start.26 = (f32[768]{0:T(1024)}, f32[768]{0:T(1024)S(1)}, u32[]{:S(2)}) copy-start(f32[768]{0:T(1024)S(1)} %get-tuple-element.86) | copy-start | bytes 9220
  165.3 77.2 %all-to-all-start.1 = ((bf16[16,128,768]{2,1,0:T(8,128)(2,1)}), bf16[16,128,768]{2,1,0:T(8,128)(2,1)S(1)}, u32[]{:S(2)}, u32[]{:S(2)}) async-start(bf16[16,128,768]{2,1,0:T(8,128)(2,1)} %bitcast.122), calls=%async_computation.1 | async-start | bytes 6291456 | tf_op jit(solution)/shard_map/all_to_all | solution.py:227
  310.5 75.2 %all-to-all-start.3 = ((bf16[16,128,768]{2,1,0:T(8,128)(2,1)}), bf16[16,128,768]{2,1,0:T(8,128)(2,1)}, u32[]{:S(2)}, u32[]{:S(2)}) async-start(bf16[16,128,768]{2,1,0:T(8,128)(2,1)} %bitcast.123), calls=%async_computation.3 | async-start | bytes 6291456 | tf_op jit(solution)/shard_map/all_to_all | solution.py:227
  385.8 75.0 %all-to-all-start.2 = ((bf16[16,128,768]{2,1,0:T(8,128)(2,1)}), bf16[16,128,768]{2,1,0:T(8,128)(2,1)}, u32[]{:S(2)}, u32[]{:S(2)}) async-start(bf16[16,128,768]{2,1,0:T(8,128)(2,1)} %bitcast.120), calls=%async_computation.2 | async-start | bytes 6291456 | tf_op jit(solution)/shard_map/all_to_all | solution.py:227
  407.2 18.4 %copy-start.46 = (s32[832]{0:T(1024)S(1)}, s32[832]{0:T(1024)}, u32[]{:S(2)}) copy-start(s32[832]{0:T(1024)} %copy-done.45) | copy-start | bytes 9988
  407.2 18.4 %copy-start.48 = (s32[832]{0:T(1024)S(1)}, s32[832]{0:T(1024)}, u32[]{:S(2)}) copy-start(s32[832]{0:T(1024)} %copy-done.47) | copy-start | bytes 9988
  407.3 132.9 %collective-permute-start.6 = (bf16[1,768,3072]{2,1,0:T(8,128)(2,1)}, bf16[1,768,3072]{2,1,0:T(8,128)(2,1)}, u32[]{:S(2)}, u32[]{:S(2)}) collective-permute-start(bf16[1,768,3072]{2,1,0:T(8,128)(2,1)} %fusion.19), channel_id=1, source_target_pairs={{0,16},{16,0},{1,17},{17,1},{2,18},{18,2},{3,19},{19,3},{4,20},{20... | collective-permute-start | bytes 14155784 | tf_op jit(solution)/shard_map/ppermute | solution.py:152
  425.5 124.0 %collective-permute-start.7 = (bf16[1,3072,768]{2,1,0:T(8,128)(2,1)}, bf16[1,3072,768]{2,1,0:T(8,128)(2,1)}, u32[]{:S(2)}, u32[]{:S(2)}) collective-permute-start(bf16[1,3072,768]{2,1,0:T(8,128)(2,1)} %fusion.18), channel_id=1, source_target_pairs={{0,16},{16,0},{1,17},{17,1},{2,18},{18,2},{3,19},{19,3},{4,20},{20... | collective-permute-start | bytes 14155784 | tf_op jit(solution)/shard_map/ppermute | solution.py:152
  479.5 4.2 collective-permute-start
  481.1 2.5 collective-permute-start.1
  485.8 25.1 %all-to-all-start.4 = ((bf16[16,48,512]{2,1,0:T(8,128)(2,1)}), bf16[16,48,512]{2,1,0:T(8,128)(2,1)S(1)}, u32[]{:S(2)}, u32[]{:S(2)}) async-start(bf16[16,48,512]{2,1,0:T(8,128)(2,1)} %bitcast.23), calls=%async_computation.4 | async-start | bytes 1572864 | tf_op jit(solution)/shard_map/all_to_all | solution.py:182
  492.2 18.7 %copy-start.19 = (bf16[832,768]{1,0:T(8,128)(2,1)S(1)}, bf16[832,768]{1,0:T(8,128)(2,1)}, u32[]{:S(2)}) copy-start(bf16[832,768]{1,0:T(8,128)(2,1)} %copy-done.18) | copy-start | bytes 3833860
  516.0 11.7 %collective-permute-start.2 = (bf16[768,1152]{1,0:T(8,128)(2,1)}, bf16[768,1152]{1,0:T(8,128)(2,1)}, u32[]{:S(2)}, u32[]{:S(2)}) collective-permute-start(bf16[768,1152]{1,0:T(8,128)(2,1)} %convolution_convert_fusion.2), channel_id=1, source_target_pairs={{0,16},{16,0},{1,17},{17,1},{2,18},{18,2},{3,19},{19,3},{4,20},{20... | collective-permute-start | bytes 5308424 | tf_op jit(solution)/shard_map/ppermute | solution.py:169
  526.2 1.5 collective-permute-start.3
  533.4 51.8 %all-to-all-start.5 = ((bf16[16,48,1280]{2,1,0:T(8,128)(2,1)}), bf16[16,48,1280]{2,1,0:T(8,128)(2,1)}, u32[]{:S(2)}, u32[]{:S(2)}) async-start(bf16[16,48,1280]{2,1,0:T(8,128)(2,1)} %bitcast.27), calls=%async_computation.5 | async-start | bytes 3932160 | tf_op jit(solution)/shard_map/all_to_all | solution.py:182
  562.2 12.3 %collective-permute-start.5 = (f32[48,384]{1,0:T(8,128)S(1)}, f32[48,384]{1,0:T(8,128)S(1)}, u32[]{:S(2)}, u32[]{:S(2)}) collective-permute-start(f32[48,384]{1,0:T(8,128)S(1)} %slice.104), channel_id=1, source_target_pairs={{0,16},{16,0},{1,17},{17,1},{2,18},{18,2},{3,19},{19,3},{4,20},{20... | collective-permute-start | bytes 221192 | tf_op jit(solution)/shard_map/ppermute | solution.py:194
  587.1 2.7 collective-permute-start.4
  (41 other events, 166.0 us)
Sparse Core Ops, SparseCore 0:
  13.0 128.9 all-gather.1

commit v3 on v2

--- a/solution.py
+++ b/solution.py
@@ -256,7 +256,6 @@
     pick_any = (in_slot[0] | in_slot[1]).astype(jnp.bfloat16)
     grad_low = pad_rows(cotangent, n_images)
     grad_slots = matmul_tn(pick_any, grad_low).astype(jnp.bfloat16)
-    gathered, grad_arrived = lax.optimization_barrier((gathered, to_expert(grad_slots)))
 
     w_qkv = gathered[:, : 3 * width]
     w_attn = gathered[:, 3 * width : 4 * width]
@@ -275,6 +274,8 @@
     mid = inputs + jnp.dot(attended, w_attn, preferred_element_type=jnp.float32)
     normed2 = layer_norm(mid, gain_two, bias_two).astype(jnp.bfloat16)
     expert_rows = to_expert(matmul_tn(pick_any, normed2).astype(jnp.bfloat16))
+    expert_rows, grad_slots = lax.optimization_barrier((expert_rows, grad_slots))
+    grad_arrived = to_expert(grad_slots)
     logits = jnp.dot(normed2, w_router, preferred_element_type=jnp.float32)
     router_probs = jax.nn.softmax(logits, axis=-1)
     onehot = (
@@ -296,6 +297,7 @@
     result_low = jnp.einsum(
         "erf,efd->erd", hidden_low, expert_out, preferred_element_type=jnp.float32
     ).astype(jnp.bfloat16)
+    result_low, grad_arrived = lax.optimization_barrier((result_low, grad_arrived))
     returned = to_tokens(result_low)
     grad_result = (gates_arrived * grad_arrived.astype(jnp.float32)).astype(jnp.bfloat16)
     grad_hidden = jnp.einsum(

time: 602 us -> 601 us (level)
  waiting for transfers between devices: 278 us -> 201 us
  blocking collectives: 0 us -> 73.9 us
  starting transfers between devices: 41.4 us -> 34.2 us
  local copies, waits for them, and re-layouts: 27.1 us -> 34 us
    all_to_all x4 -> x3, waiting for transfers between devices: 256 us -> 112 us  [exchange(): lax.all_to_all(slots.reshape(num_experts, capacity, -1), 'exp', split_axi...]
    all_to_all x0 -> x1, blocking collectives: none -> 73.9 us  [exchange(): lax.all_to_all(slots.reshape(num_experts, capacity, -1), 'exp', split_axi...]
    all_gather x1, waiting for transfers between devices: 9.66 us -> 76.4 us  [on_device(): gathered = lax.all_gather(packed, 'exp', axis=0, tiled=True)]
    all_to_all x4 -> x3, starting transfers between devices: 23.4 us -> 15.7 us  [exchange(): lax.all_to_all(slots.reshape(num_experts, capacity, -1), 'exp', split_axi...]
    dot_general x1, matrix products: 15.9 us -> 23.2 us  [on_device(): jnp.einsum('erf,edf->erd', grad_pre, expert_in, preferred_element_type=jn...]
    unnamed x100 -> x102, local copies, waits for them, and re-layouts: 10.5 us -> 13.8 us
  transfers between devices with their start and end apart: 15 -> 14, of which waited for: 7 -> 6; matrix products, arithmetic and copies ran while one was open for 23% -> 29% of each run, Pallas kernels for 3% -> 3%
where the time goes in v3:
time: 601 us; the launch traced here: 597 us
  waiting for transfers between devices  201 us (33%)
  matrix products  174 us (29%)
  blocking collectives  73.9 us (12%)
  other arithmetic  40.4 us (7%)
  starting transfers between devices  34.2 us (6%)
  local copies, waits for them, and re-layouts  34 us (6%)
  Pallas kernels  23.9 us (4%)
  between operations  15.2 us (3%)
    all_to_all x3, waiting for transfers between devices, exchange(): lax.all_to_all(slots.reshape(num_experts, capacity, -1), 'exp', split_axi...  112 us
    all_gather x1, waiting for transfers between devices, on_device(): gathered = lax.all_gather(packed, 'exp', axis=0, tiled=True)  76.4 us
    all_to_all x1, blocking collectives, exchange(): lax.all_to_all(slots.reshape(num_experts, capacity, -1), 'exp', split_axi...  73.9 us
    dot_general x1, matrix products, on_device(): jnp.einsum('erd,edf->erf', expert_rows, expert_in, preferred_element_type...  32.9 us
    pallas_call x2, Pallas kernels, per_image(): pl.pallas_call(kernel, grid=(n_images,), in_specs=[pl.BlockSpec((1, SEQ_P...  23.9 us
    dot_general x7, matrix products, matmul_tn(): lax.dot_general(left, right, (((0,), (0,)), ((), ())), preferred_element_...  23.4 us
    dot_general x1, matrix products, on_device(): jnp.einsum('erf,edf->erd', grad_pre, expert_in, preferred_element_type=jn...  23.2 us
    add x2, other arithmetic, sum_replicas(): return low.astype(jnp.float32) + other.astype(jnp.float32)  18 us
  transfers between devices with their start and end apart: 14, of which 6 were waited for; matrix products, arithmetic and copies ran while one was open for 29% of the time, Pallas kernels for 3%

profile of v3, /device:TPU:13, one launch (start us, length us, event | category | flops | bytes accessed | tf_op | source)
XLA Modules:
  0.0 596.7 jit_solution(15627528036727932319)
XLA Ops:
  18.5 76.4 %all-gather.2.cloned.1.call-done = bf16[768,3200]{1,0:T(8,128)(2,1)} async-done(((bf16[48,3200]{1,0:T(8,128)(2,1)}), bf16[768,3200]{1,0:T(8,128)(2,1)}) %all-gather.2.cloned.1.call-update) | async-done | bytes 4915216 | tf_op jit(solution)/shard_map/all_gather | solution.py:248
  101.8 7.1 %shard_map.221 = bf16[4,208,768]{2,1,0:T(8,128)(2,1)S(1)} custom-call(bf16[4,208,2304]{2,1,0:T(8,128)(2,1)S(1)} %bitcast.114), custom_call_target="tpu_custom_call" | custom-call | flops 8000000000 | bytes 8000000 | tf_op jit(solution)/shard_map/pallas_call | solution.py:110
  112.1 6.1 %fusion.44 = bf16[2048,768]{1,0:T(8,128)(2,1)} fusion(bf16[832,768]{1,0:T(8,128)(2,1)S(1)} %add_convert_fusion.3, s32[832]{0:T(1024)S(1)} %get-tuple-element.103, s32[832]{0:T(1024)S(1)} %get-tuple-element.102), kind=kOutput, calls=%fused_computation.50 | convolution fusion | flops 2623930368 | bytes 4430336 | tf_op jit(solution)/shard_map/dot_general | solution.py:42
  118.2 5.8 all-to-all-start
  129.1 6.1 %fusion.47 = bf16[2048,768]{1,0:T(8,128)(2,1)} fusion(bf16[832,768]{1,0:T(8,128)(2,1)S(1)} %bitcast.128, s32[832]{0:T(1024)S(1)} %get-tuple-element.103, s32[832]{0:T(1024)S(1)} %get-tuple-element.102), kind=kOutput, calls=%fused_computation.51 | convolution fusion | flops 2623930368 | bytes 4430336 | tf_op jit(solution)/shard_map/dot_general | solution.py:42
  135.2 59.2 %all-to-all-done = bf16[16,128,768]{2,1,0:T(8,128)(2,1)S(1)} async-done(((bf16[16,128,768]{2,1,0:T(8,128)(2,1)}), bf16[16,128,768]{2,1,0:T(8,128)(2,1)S(1)}, u32[]{:S(2)}, u32[]{:S(2)}) %all-to-all-start) | async-done | bytes 3145760 | tf_op jit(solution)/shard_map/all_to_all | solution.py:227
  199.1 32.9 %fusion.5 = (bf16[1,2048,3072]{2,1,0:T(8,128)(2,1)}, bf16[2048,3072]{1,0:T(8,128)(2,1)S(1)}) fusion(bf16[1,768,3072]{2,1,0:T(8,128)(2,1)} %param.22, bf16[1,2048,768]{2,1,0:T(8,128)(2,1)S(1)} %bitcast.125), kind=kOutput, calls=%fused_computation.10 | convolution fusion | flops 9833545728 | bytes 33030144 | tf_op jit(solution)/shard_map/erd,edf->erf/dot_general | solution.py:293
  236.6 13.5 %fusion.58 = bf16[1,2048,768]{2,1,0:T(8,128)(2,1)} fusion(bf16[2048,3072]{1,0:T(8,128)(2,1)S(1)} %get-tuple-element.107, bf16[1,3072,768]{2,1,0:T(8,128)(2,1)} %param.23), kind=kOutput, calls=%fused_computation.62 | convolution fusion | flops 9665249280 | bytes 20447232 | tf_op jit(solution)/shard_map/erf,efd->erd/dot_general | solution.py:297
  250.2 19.5 %all-to-all-done.1 = bf16[16,128,768]{2,1,0:T(8,128)(2,1)} async-done(((bf16[16,128,768]{2,1,0:T(8,128)(2,1)}), bf16[16,128,768]{2,1,0:T(8,128)(2,1)}, u32[]{:S(2)}, u32[]{:S(2)}) %all-to-all-start.1) | async-done | bytes 3145760 | tf_op jit(solution)/shard_map/all_to_all | solution.py:227
  269.6 17.4 %fusion = bf16[1,2048,3072]{2,1,0:T(8,128)(2,1)} fusion(bf16[1,2048,3072]{2,1,0:T(8,128)(2,1)} %get-tuple-element.106, bf16[1,3072,768]{2,1,0:T(8,128)(2,1)} %param.23, bf16[1,2048,768]{2,1,0:T(8,128)(2,1)} %bitcast.15, f32[2048]{0:T(1024)S(1)} %select_reduce_fusion), kind=kOutput, calls=%fused_computation.2 | convolution fusion | flops 9687269376 | bytes 33038336 | tf_op jit(solution)/shard_map/erd,efd->erf/dot_general | solution.py:303
  287.1 23.2 %fusion.39 = bf16[2048,768]{1,0:T(8,128)(2,1)S(1)} fusion(bf16[1,768,3072]{2,1,0:T(8,128)(2,1)} %param.22, bf16[1,2048,3072]{2,1,0:T(8,128)(2,1)} %fusion), kind=kOutput, calls=%fused_computation.49 | convolution fusion | flops 9665249280 | bytes 20447232 | tf_op jit(solution)/shard_map/erf,edf->erd/dot_general | solution.py:307
  310.3 73.9 %all_to_all.30 = bf16[16,128,768]{2,1,0:T(8,128)(2,1)} all-to-all(bf16[16,128,768]{2,1,0:T(8,128)(2,1)S(1)} %bitcast.136), channel_id=1, replica_groups=mesh['rep'=2,'exp'=16] {'exp'}, dimensions={0} | all-to-all | bytes 6291456 | tf_op jit(solution)/shard_map/all_to_all | solution.py:227
  384.2 5.0 all-to-all-start.2
  391.7 16.0 %fusion.18 = bf16[1,3072,768]{2,1,0:T(8,128)(2,1)} fusion(bf16[2048,3072]{1,0:T(8,128)(2,1)} %copy-done.46, bf16[1,2048,768]{2,1,0:T(8,128)(2,1)} %bitcast.15, f32[2048]{0:T(1024)S(1)} %select_reduce_fusion), kind=kOutput, calls=%fused_computation.28 | convolution fusion | flops 9670754304 | bytes 20455424 | tf_op jit(solution)/shard_map/erf,erd->efd/dot_general | solution.py:311
  407.8 11.9 %fusion.19 = bf16[1,768,3072]{2,1,0:T(8,128)(2,1)} fusion(bf16[1,2048,3072]{2,1,0:T(8,128)(2,1)S(1)} %bitcast.142, bf16[1,2048,768]{2,1,0:T(8,128)(2,1)S(1)} %bitcast.127), kind=kOutput, calls=%fused_computation.29 | convolution fusion | flops 9666035712 | bytes 20447232 | tf_op jit(solution)/shard_map/erd,erf->edf/dot_general | solution.py:314
  425.9 33.8 %all-to-all-done.2 = bf16[16,128,768]{2,1,0:T(8,128)(2,1)} async-done(((bf16[16,128,768]{2,1,0:T(8,128)(2,1)}), bf16[16,128,768]{2,1,0:T(8,128)(2,1)}, u32[]{:S(2)}, u32[]{:S(2)}) %all-to-all-start.2) | async-done | bytes 3145760 | tf_op jit(solution)/shard_map/all_to_all | solution.py:227
  464.9 5.3 fusion.61
  491.1 16.8 %shard_map.222 = bf16[4,208,2304]{2,1,0:T(8,128)(2,1)S(1)} custom-call(bf16[4,208,2304]{2,1,0:T(8,128)(2,1)S(1)} %bitcast.115, bf16[4,208,768]{2,1,0:T(8,128)(2,1)S(1)} %bitcast.122), custom_call_target="tpu_custom_call" | custom-call | flops 20000000000 | bytes 8000000 | tf_op jit(solution)/shard_map/pallas_call | solution.py:110
  509.9 5.1 convolution_convert_fusion.2
  516.1 8.5 %multiply_reduce_fusion = (bf16[768]{0:T(1024)(128)(2,1)S(1)}, f32[832]{0:T(1024)S(1)}, bf16[768]{0:T(1024)(128)(2,1)S(1)}, f32[832,768]{1,0:T(8,128)}) fusion(f32[832]{0:T(1024)S(1)} %copy-done.39, f32[832]{0:T(1024)S(1)} %copy-done.37, f32[4,208,768]{2,1,0:T(8,128)} %copy-done.10, f32[768]{0:T(1024)S(1)} %copy-done.35, f32[832,768]{1,0:T(8,128)} %bitcast.124, ...), kind=kOutput, calls=%fused_computation.65 | convolution fusion | flops 2950149888 | bytes 15056640 | tf_op jit(solution)/shard_map/dot_general | solution.py:48
  532.3 6.7 %all-to-all-start.5 = ((bf16[16,48,1280]{2,1,0:T(8,128)(2,1)}), bf16[16,48,1280]{2,1,0:T(8,128)(2,1)}, u32[]{:S(2)}, u32[]{:S(2)}) async-start(bf16[16,48,1280]{2,1,0:T(8,128)(2,1)} %bitcast.29), calls=%async_computation.5 | async-start | bytes 3932160 | tf_op jit(solution)/shard_map/all_to_all | solution.py:182
  539.1 9.4 %convert_add_fusion.1 = f32[1,768,3072]{2,1,0:T(8,128)} fusion(bf16[1,768,3072]{2,1,0:T(8,128)(2,1)} %collective-permute-done.6, bf16[1,768,3072]{2,1,0:T(8,128)(2,1)} %fusion.19), kind=kLoop, calls=%fused_computation.12 | loop fusion | flops 7077888 | bytes 18874368 | tf_op jit(solution)/shard_map/add | solution.py:153
  548.4 8.6 %convert_add_fusion = f32[1,3072,768]{2,1,0:T(8,128)} fusion(bf16[1,3072,768]{2,1,0:T(8,128)(2,1)} %collective-permute-done.7, bf16[1,3072,768]{2,1,0:T(8,128)(2,1)} %fusion.18), kind=kLoop, calls=%fused_computation.11 | loop fusion | flops 7077888 | bytes 18874368 | tf_op jit(solution)/shard_map/add | solution.py:153
  573.4 10.7 %all-to-all-done.5 = bf16[16,48,1280]{2,1,0:T(8,128)(2,1)} async-done(((bf16[16,48,1280]{2,1,0:T(8,128)(2,1)}), bf16[16,48,1280]{2,1,0:T(8,128)(2,1)}, u32[]{:S(2)}, u32[]{:S(2)}) %all-to-all-start.5) | async-done | bytes 1966112 | tf_op jit(solution)/shard_map/all_to_all | solution.py:182
  (223 shorter events, 102.4 us)
Async XLA Ops:
  7.2 87.8 %all-gather.2.cloned.1.call-start = ((), (), s32[]{:S(2)}) async-start(), calls=%async_computation.6 | async-start | bytes 5222400 | tf_op jit(solution)/shard_map/all_gather | solution.py:248
  15.8 81.1 %copy-start.36 = (f32[832]{0:T(1024)}, f32[832]{0:T(1024)S(1)}, u32[]{:S(2)}) copy-start(f32[832]{0:T(1024)S(1)} %div.64) | copy-start | bytes 9988
  17.0 79.9 %copy-start.38 = (f32[832]{0:T(1024)}, f32[832]{0:T(1024)S(1)}, u32[]{:S(2)}) copy-start(f32[832]{0:T(1024)S(1)} %rsqrt.22) | copy-start | bytes 9988
  17.0 111.1 %copy-start.42 = (s32[832]{0:T(1024)}, s32[832]{0:T(1024)S(1)}, u32[]{:S(2)}) copy-start(s32[832]{0:T(1024)S(1)} %get-tuple-element.102) | copy-start | bytes 9988
  17.0 111.1 %copy-start.44 = (s32[832]{0:T(1024)}, s32[832]{0:T(1024)S(1)}, u32[]{:S(2)}) copy-start(s32[832]{0:T(1024)S(1)} %get-tuple-element.103) | copy-start | bytes 9988
  18.5 90.4 %copy-start.10 = (f32[4,208,768]{2,1,0:T(8,128)}, f32[4,208,768]{2,1,0:T(8,128)S(1)}, u32[]{:S(2)}) copy-start(f32[4,208,768]{2,1,0:T(8,128)S(1)} %pad_convert_fusion) | copy-start | bytes 7667716
  96.8 14.8 %copy-start.26 = (f32[768]{0:T(1024)}, f32[768]{0:T(1024)S(1)}, u32[]{:S(2)}) copy-start(f32[768]{0:T(1024)S(1)} %get-tuple-element.90) | copy-start | bytes 9220
  118.2 76.1 %all-to-all-start = ((bf16[16,128,768]{2,1,0:T(8,128)(2,1)}), bf16[16,128,768]{2,1,0:T(8,128)(2,1)S(1)}, u32[]{:S(2)}, u32[]{:S(2)}) async-start(bf16[16,128,768]{2,1,0:T(8,128)(2,1)} %bitcast.135), calls=%async_computation | async-start | bytes 6291456 | tf_op jit(solution)/shard_map/all_to_all | solution.py:227
  194.3 75.3 %all-to-all-start.1 = ((bf16[16,128,768]{2,1,0:T(8,128)(2,1)}), bf16[16,128,768]{2,1,0:T(8,128)(2,1)}, u32[]{:S(2)}, u32[]{:S(2)}) async-start(bf16[16,128,768]{2,1,0:T(8,128)(2,1)} %bitcast.134), calls=%async_computation.1 | async-start | bytes 6291456 | tf_op jit(solution)/shard_map/all_to_all | solution.py:227
  384.2 75.6 %all-to-all-start.2 = ((bf16[16,128,768]{2,1,0:T(8,128)(2,1)}), bf16[16,128,768]{2,1,0:T(8,128)(2,1)}, u32[]{:S(2)}, u32[]{:S(2)}) async-start(bf16[16,128,768]{2,1,0:T(8,128)(2,1)} %bitcast.132), calls=%async_computation.2 | async-start | bytes 6291456 | tf_op jit(solution)/shard_map/all_to_all | solution.py:227
  389.7 18.0 %slice-start.1 = ((s8[12582912]{0:T(1024)(128)(4,1)}), s8[4194304]{0:T(1024)(128)(4,1)S(1)}, s32[]{:S(2)}) async-start(s8[12582912]{0:T(1024)(128)(4,1)} %bitcast.141), calls=%async_computation.8 | async-start | bytes 8388608
  391.7 16.1 %slice-start.2 = ((s8[12582912]{0:T(1024)(128)(4,1)}), s8[4194304]{0:T(1024)(128)(4,1)S(1)}, s32[]{:S(2)}) async-start(s8[12582912]{0:T(1024)(128)(4,1)} %bitcast.141), calls=%async_computation.9 | async-start | bytes 8388608
  391.7 16.0 %slice-start.3 = ((s8[12582912]{0:T(1024)(128)(4,1)}), s8[4194304]{0:T(1024)(128)(4,1)S(1)}, s32[]{:S(2)}) async-start(s8[12582912]{0:T(1024)(128)(4,1)} %bitcast.141), calls=%async_computation.10 | async-start | bytes 8388608
  419.7 119.3 %collective-permute-start.6 = (bf16[1,768,3072]{2,1,0:T(8,128)(2,1)}, bf16[1,768,3072]{2,1,0:T(8,128)(2,1)}, u32[]{:S(2)}, u32[]{:S(2)}) collective-permute-start(bf16[1,768,3072]{2,1,0:T(8,128)(2,1)} %fusion.19), channel_id=1, source_target_pairs={{0,16},{16,0},{1,17},{17,1},{2,18},{18,2},{3,19},{19,3},{4,20},{20... | collective-permute-start | bytes 14155784 | tf_op jit(solution)/shard_map/ppermute | solution.py:152
  422.3 126.1 %collective-permute-start.7 = (bf16[1,3072,768]{2,1,0:T(8,128)(2,1)}, bf16[1,3072,768]{2,1,0:T(8,128)(2,1)}, u32[]{:S(2)}, u32[]{:S(2)}) collective-permute-start(bf16[1,3072,768]{2,1,0:T(8,128)(2,1)} %fusion.18), channel_id=1, source_target_pairs={{0,16},{16,0},{1,17},{17,1},{2,18},{18,2},{3,19},{19,3},{4,20},{20... | collective-permute-start | bytes 14155784 | tf_op jit(solution)/shard_map/ppermute | solution.py:152
  478.4 4.2 collective-permute-start
  480.1 2.5 collective-permute-start.1
  484.8 25.1 %all-to-all-start.4 = ((bf16[16,48,512]{2,1,0:T(8,128)(2,1)}), bf16[16,48,512]{2,1,0:T(8,128)(2,1)S(1)}, u32[]{:S(2)}, u32[]{:S(2)}) async-start(bf16[16,48,512]{2,1,0:T(8,128)(2,1)} %bitcast.25), calls=%async_computation.4 | async-start | bytes 1572864 | tf_op jit(solution)/shard_map/all_to_all | solution.py:182
  491.1 18.7 %copy-start.20 = (bf16[832,768]{1,0:T(8,128)(2,1)S(1)}, bf16[832,768]{1,0:T(8,128)(2,1)}, u32[]{:S(2)}) copy-start(bf16[832,768]{1,0:T(8,128)(2,1)} %copy-done.19) | copy-start | bytes 3833860
  515.0 11.7 %collective-permute-start.2 = (bf16[768,1152]{1,0:T(8,128)(2,1)}, bf16[768,1152]{1,0:T(8,128)(2,1)}, u32[]{:S(2)}, u32[]{:S(2)}) collective-permute-start(bf16[768,1152]{1,0:T(8,128)(2,1)} %convolution_convert_fusion.2), channel_id=1, source_target_pairs={{0,16},{16,0},{1,17},{17,1},{2,18},{18,2},{3,19},{19,3},{4,20},{20... | collective-permute-start | bytes 5308424 | tf_op jit(solution)/shard_map/ppermute | solution.py:169
  525.0 1.5 collective-permute-start.3
  532.3 51.8 %all-to-all-start.5 = ((bf16[16,48,1280]{2,1,0:T(8,128)(2,1)}), bf16[16,48,1280]{2,1,0:T(8,128)(2,1)}, u32[]{:S(2)}, u32[]{:S(2)}) async-start(bf16[16,48,1280]{2,1,0:T(8,128)(2,1)} %bitcast.29), calls=%async_computation.5 | async-start | bytes 3932160 | tf_op jit(solution)/shard_map/all_to_all | solution.py:182
  561.1 12.3 %collective-permute-start.5 = (f32[48,384]{1,0:T(8,128)S(1)}, f32[48,384]{1,0:T(8,128)S(1)}, u32[]{:S(2)}, u32[]{:S(2)}) collective-permute-start(f32[48,384]{1,0:T(8,128)S(1)} %slice.108), channel_id=1, source_target_pairs={{0,16},{16,0},{1,17},{17,1},{2,18},{18,2},{3,19},{19,3},{4,20},{20... | collective-permute-start | bytes 221192 | tf_op jit(solution)/shard_map/ppermute | solution.py:194
  586.0 2.7 collective-permute-start.4
  (41 other events, 197.5 us)
Sparse Core Ops, SparseCore 0:
  13.0 81.9 all-gather.1
